TPU v7x, 256 devices: a whole 4x4x8 slice. The times are simulated.
256 devices in a mesh: axial: 8 (over x, core), trans: 32 (over z, y).
Axes of the slice: x: 4, y: 4, z: 8, core: 2. Of those that a mesh axis runs over, the one named last changes fastest.
Arguments:
- start_modes: float32 [16, 3, 16, 256, 128], P(None, None, 'axial', 'trans'), may hold values from -40 to 40
- region: int32 [16, 256, 128], P('axial', 'trans'), may hold values from 0 to 3
- edge_mask: int32 [3, 16, 256, 128], P(None, 'axial', 'trans'), may hold values 0 or 1
- reluctivity: float32 [4], replicated, may hold values from 0.5 to 2
- permittivity: float32 [4], replicated, may hold values from 1 to 4
- block_inverse: float32 [12, 48, 8, 128, 128], P(None, None, 'axial', 'trans'), may hold values from -0.08 to 2.08
Outputs:
- modes: float32 [16, 3, 16, 256, 128], P(None, None, 'axial', 'trans')
- residual: float32 [16, 3, 16, 256, 128], P(None, None, 'axial', 'trans')
All inputs are finite; a program needn't handle non-finite values. No bound on the sum of `edge_mask` on one device may be relied on, other than what follows from the above.
Results may differ from a plain program's by a relative error of at most 0.0003.
Values sent between devices are 32-bit elements; how exact they have to be, the bound alone decides.
A program may use at most 64 MiB of HBM per device.

v0:
```python
import jax
import jax.numpy as jnp
from jax import lax
from jax.sharding import PartitionSpec as P

V = 16
ITERS = 2
INNER = 3


highest = lax.Precision.HIGHEST


def from_behind(value, axis, steps):
    count = lax.axis_size(axis)
    first, last = (max(0, -steps), min(count, count - steps))
    return lax.ppermute(value, axis, [(source, source + steps) for source in range(first, last)])


def extended(x, sides, width):
    for axis, dim in sides:
        size, length = (lax.axis_size(axis), x.shape[dim])
        up = [(i, (i + 1) % size) for i in range(size - 1)]
        down = [(j, i) for i, j in up]
        last = lax.slice_in_dim(x, length - width, length, axis=dim)
        first = lax.slice_in_dim(x, 0, width, axis=dim)
        before = lax.ppermute(last, axis, up)
        after = lax.ppermute(first, axis, down)
        x = jnp.concatenate([before, x, after], axis=dim)
    return x


def window_view(source, shift_x, shift_y, shift_z):
    return source[
        ...,
        shift_x : source.shape[-3] - 1 + shift_x,
        shift_y : source.shape[-2] - 1 + shift_y,
        shift_z : source.shape[-1] - 1 + shift_z,
    ]


def behind_view(source, shift_x, shift_y, shift_z):
    return source[
        ...,
        1 - shift_x : source.shape[-3] - shift_x,
        1 - shift_y : source.shape[-2] - shift_y,
        1 - shift_z : source.shape[-1] - shift_z,
    ]


def curl_curl(padded, weight_pad):
    field_x = padded[..., 0, :, :, :]
    field_y = padded[..., 1, :, :, :]
    field_z = padded[..., 2, :, :, :]
    weight = window_view(weight_pad, 0, 0, 0)
    flux_x = weight * (
        window_view(field_z, 0, 1, 0)
        - window_view(field_z, 0, 0, 0)
        - window_view(field_y, 0, 0, 1)
        + window_view(field_y, 0, 0, 0)
    )
    flux_y = weight * (
        window_view(field_x, 0, 0, 1)
        - window_view(field_x, 0, 0, 0)
        - window_view(field_z, 1, 0, 0)
        + window_view(field_z, 0, 0, 0)
    )
    flux_z = weight * (
        window_view(field_y, 1, 0, 0)
        - window_view(field_y, 0, 0, 0)
        - window_view(field_x, 0, 1, 0)
        + window_view(field_x, 0, 0, 0)
    )
    node_div = (
        window_view(field_x, 1, 1, 1)
        - window_view(field_x, 0, 1, 1)
        + window_view(field_y, 1, 1, 1)
        - window_view(field_y, 1, 0, 1)
        + window_view(field_z, 1, 1, 1)
        - window_view(field_z, 1, 1, 0)
    )
    curl_x = (
        behind_view(flux_z, 0, 0, 0)
        - behind_view(flux_z, 0, 1, 0)
        - behind_view(flux_y, 0, 0, 0)
        + behind_view(flux_y, 0, 0, 1)
        + window_view(node_div, 0, 0, 0)
        - window_view(node_div, 1, 0, 0)
    )
    curl_y = (
        behind_view(flux_x, 0, 0, 0)
        - behind_view(flux_x, 0, 0, 1)
        - behind_view(flux_z, 0, 0, 0)
        + behind_view(flux_z, 1, 0, 0)
        + window_view(node_div, 0, 0, 0)
        - window_view(node_div, 0, 1, 0)
    )
    curl_z = (
        behind_view(flux_y, 0, 0, 0)
        - behind_view(flux_y, 1, 0, 0)
        - behind_view(flux_x, 0, 0, 0)
        + behind_view(flux_x, 0, 1, 0)
        + window_view(node_div, 0, 0, 0)
        - window_view(node_div, 0, 0, 1)
    )
    return jnp.stack([curl_x, curl_y, curl_z], axis=-4)


def material_value(region, level_table):
    levels = jnp.arange(level_table.shape[0], dtype=jnp.int32)
    selected = (region[None] == levels[:, None, None, None]).astype(jnp.float32)
    return jnp.sum(selected * level_table[:, None, None, None], axis=0)


def block_solve(padded, block_inverse):
    vectors = padded.shape[0]
    size_x = padded.shape[-3] - 2
    size_y = padded.shape[-2] - 2
    size_z = padded.shape[-1]
    pieces = []
    for offset_x in range(4):
        for offset_y in range(4):
            pieces.append(
                padded[:, :, offset_x : offset_x + size_x : 2, offset_y : offset_y + size_y : 2, :]
            )
    patches = jnp.stack(pieces, axis=2).reshape(vectors, 48, size_x // 2, size_y // 2, size_z)
    result = jnp.einsum("abxyz,vbxyz->vaxyz", block_inverse, patches, precision=highest)
    result = result.reshape(vectors, 3, 2, 2, size_x // 2, size_y // 2, size_z)
    return result.transpose(0, 1, 4, 2, 5, 3, 6).reshape(vectors, 3, size_x, size_y, size_z)


def mass_terms(blocks, permittivity_cell):
    flattened = [member.reshape(member.shape[0], -1) for member in blocks]
    weighted = [(member * permittivity_cell).reshape(member.shape[0], -1) for member in blocks]
    return jnp.concatenate(
        [
            jnp.concatenate(
                [jnp.dot(row_block, col_block.T, precision=highest) for col_block in weighted],
                axis=1,
            )
            for row_block in flattened
        ],
        axis=0,
    )


def stiff_terms(blocks, images):
    flattened = [member.reshape(member.shape[0], -1) for member in blocks]
    imaged = [member.reshape(member.shape[0], -1) for member in images]
    return jnp.concatenate(
        [
            jnp.concatenate(
                [jnp.dot(row_block, col_block.T, precision=highest) for col_block in imaged], axis=1
            )
            for row_block in flattened
        ],
        axis=0,
    )


def combine(coeffs, blocks):
    block_rows = blocks[0].shape[0]
    summed = jnp.tensordot(coeffs[:block_rows], blocks[0], axes=([0], [0]), precision=highest)
    for position in range(1, len(blocks)):
        summed = summed + jnp.tensordot(
            coeffs[position * block_rows : (position + 1) * block_rows],
            blocks[position],
            axes=([0], [0]),
            precision=highest,
        )
    return summed


def residual_block(images, mode_block, rayleigh, permittivity_cell):
    return images - permittivity_cell * jnp.tensordot(
        rayleigh, mode_block, axes=([0], [0]), precision=highest
    )


def rayleigh_ritz(mass_matrix, stiff_matrix, wanted, inner_steps):
    mass_factor = jnp.linalg.cholesky(mass_matrix)
    half_solved = lax.linalg.triangular_solve(mass_factor, stiff_matrix, left_side=True, lower=True)
    projected = lax.linalg.triangular_solve(
        mass_factor, half_solved, left_side=False, lower=True, transpose_a=True
    )
    projected = 0.5 * (projected + projected.T)
    factor = jnp.linalg.cholesky(projected)
    subspace = jnp.eye(mass_matrix.shape[0], wanted, dtype=jnp.float32)
    for repeat in range(inner_steps):
        subspace = lax.linalg.triangular_solve(factor, subspace, left_side=True, lower=True)
        subspace = lax.linalg.triangular_solve(
            factor, subspace, left_side=True, lower=True, transpose_a=True
        )
        normal = jnp.linalg.cholesky(jnp.dot(subspace.T, subspace, precision=highest))
        subspace = lax.linalg.triangular_solve(
            normal, subspace, left_side=False, lower=True, transpose_a=True
        )
    coeffs = lax.linalg.triangular_solve(
        mass_factor, subspace, left_side=True, lower=True, transpose_a=True
    )
    rayleigh = jnp.dot(
        subspace.T, jnp.dot(projected, subspace, precision=highest), precision=highest
    )
    return (coeffs, rayleigh)


def start_block(mass_start, stiff_start, mode_block, images):
    mass_factor = jnp.linalg.cholesky(mass_start)
    unwind = lax.linalg.triangular_solve(
        mass_factor,
        jnp.eye(mass_start.shape[0], dtype=jnp.float32),
        left_side=True,
        lower=True,
        transpose_a=True,
    )
    mode_block = jnp.tensordot(unwind, mode_block, axes=([0], [0]), precision=highest)
    images = jnp.tensordot(unwind, images, axes=([0], [0]), precision=highest)
    rayleigh = jnp.dot(unwind.T, jnp.dot(stiff_start, unwind, precision=highest), precision=highest)
    return (mode_block, images, rayleigh)


def on_device(start_modes, region, edge_mask, reluctivity, permittivity, block_inverse):
    edge_keep = edge_mask.astype(jnp.float32)
    cell_count = (
        region.shape[0]
        * region.shape[1]
        * region.shape[2]
        * lax.axis_size("axial")
        * lax.axis_size("trans")
    )
    weight_core = material_value(region, reluctivity)
    size_x, size_y, size_z = weight_core.shape
    lower_axial = from_behind(weight_core[-1:], "axial", 1)
    lower_trans = from_behind(weight_core[:, -1:], "trans", 1)
    rows_full = jnp.concatenate(
        [lower_axial, weight_core, jnp.zeros((1, size_y, size_z), jnp.float32)], axis=0
    )
    left_column = jnp.concatenate(
        [
            jnp.zeros((1, 1, size_z), jnp.float32),
            lower_trans,
            jnp.zeros((1, 1, size_z), jnp.float32),
        ],
        axis=0,
    )
    weight_rim = jnp.concatenate(
        [left_column, rows_full, jnp.zeros((size_x + 2, 1, size_z), jnp.float32)], axis=1
    )
    weight_pad = jnp.pad(weight_rim, ((0, 0), (0, 0), (1, 1)))
    permittivity_cell = material_value(region, permittivity)

    def operate(fields):
        widened = extended(fields * edge_keep, (("axial", 2), ("trans", 3)), 1)
        padded = jnp.pad(widened, ((0, 0), (0, 0), (0, 0), (0, 0), (1, 1)))
        return edge_keep * curl_curl(padded, weight_pad)

    mode_block = edge_keep * start_modes
    images = operate(mode_block)
    mass_start, stiff_start = lax.psum(
        (mass_terms([mode_block], permittivity_cell), stiff_terms([mode_block], [images])),
        ("axial", "trans"),
    )
    mode_block, images, rayleigh = start_block(
        mass_start / cell_count, stiff_start / cell_count, mode_block, images
    )
    search = None
    search_images = None
    for sweep_index in range(ITERS):
        final_sweep = sweep_index == ITERS - 1
        residual_now = residual_block(images, mode_block, rayleigh, permittivity_cell)
        precondition_widened = extended(residual_now, (("axial", 2), ("trans", 3)), 1)
        corrected = edge_keep * block_solve(precondition_widened, block_inverse)
        blocks = [mode_block, corrected]
        if search is not None:
            blocks = blocks + [search]
        mass_matrix = lax.psum(mass_terms(blocks, permittivity_cell), ("axial", "trans"))
        corrected_images = operate(corrected)
        block_images = [images, corrected_images]
        if search is not None:
            block_images = block_images + [search_images]
        stiff_matrix = lax.psum(stiff_terms(blocks, block_images), ("axial", "trans"))
        coeffs, rayleigh = rayleigh_ritz(
            mass_matrix / cell_count, stiff_matrix / cell_count, V, INNER
        )
        new_modes = combine(coeffs, blocks)
        images = combine(coeffs, block_images)
        if not final_sweep:
            search = combine(coeffs[V:], blocks[1:])
            search_images = combine(coeffs[V:], block_images[1:])
        mode_block = new_modes
    residual_out = residual_block(images, mode_block, rayleigh, permittivity_cell)
    return (mode_block, residual_out)


def solution(mesh):
    in_specs = (
        P(None, None, "axial", "trans", None),
        P("axial", "trans", None),
        P(None, "axial", "trans", None),
        P(),
        P(),
        P(None, None, "axial", "trans", None),
    )
    out_specs = (P(None, None, "axial", "trans", None), P(None, None, "axial", "trans", None))
    return jax.shard_map(
        on_device, mesh=mesh, in_specs=in_specs, out_specs=out_specs, check_vma=False
    )
```

profile of v0, /device:TPU:1, one launch (start us, length us, event | category | flops | bytes accessed | tf_op | source)
XLA Modules:
  0.0 492.2 jit_solution(11696514057921476057)
XLA Ops:
  2.6 4.5 collective-permute-start.2
  7.1 1.9 collective-permute-start.3
  9.2 3.6 collective-permute-start.1
  12.8 3.2 collective-permute-start
  17.0 3.4 collective-permute-start.4
  20.5 1.3 collective-permute-start.5
  22.8 3.8 collective-permute-done.5
  29.2 85.4 %all-reduce.6 = (f32[16,16]{0,1:T(8,128)S(1)}, f32[16,16]{0,1:T(8,128)S(1)}) all-reduce(f32[16,16]{0,1:T(8,128)S(1)} %convolution_bitcast_fusion.38, f32[16,16]{0,1:T(8,128)S(1)} %convolution_bitcast_fusion.36), channel_id=1, replica_groups=mesh['axial'=8,'trans'=32] {'axial','trans'}, use_global_device_ids=true, to_apply=%region_1.2 | all-reduce | flops 512 | bytes 4096 | tf_op jit(solution)/shard_map/psum | solution.py:259
  114.7 1.5 cholesky.203
  117.5 1.2 custom-call.37
  120.9 2.7 collective-permute-start.6
  123.6 3.8 copy.175
  127.4 1.9 collective-permute-start.7
  130.0 4.4 collective-permute-done.7
  134.4 1.6 collective-permute-start.8
  136.0 1.8 collective-permute-start.9
  138.4 3.0 collective-permute-done.9
  141.7 2.1 copy.173
  143.8 3.9 copy.174
  147.8 12.2 %convolution_bitcast_fusion.1 = f32[16,12,1,4,128]{1,0,4,3,2:T(8,128)} fusion(f32[16,48,4,128]{1,0,3,2:T(8,128)} %copy.174, f32[12,48,4,128]{1,0,3,2:T(8,128)} %copy.175), kind=kOutput, calls=%fused_computation.3 | convolution fusion | flops 56623104 | bytes 3145728 | tf_op jit(solution)/shard_map/abxyz,vbxyz->vaxyz/dot_general | solution.py:127
  160.0 3.2 copy.176
  164.7 3.5 collective-permute-start.10
  168.1 1.9 collective-permute-start.11
  171.5 3.7 collective-permute-done.11
  175.2 3.5 collective-permute-start.12
  178.7 1.5 collective-permute-start.13
  180.3 3.7 collective-permute-done.13
  187.4 82.2 %all-reduce.5 = (f32[32,32]{0,1:T(8,128)S(1)}, f32[32,32]{0,1:T(8,128)S(1)}) all-reduce(f32[32,32]{0,1:T(8,128)S(1)} %maximum_maximum_fusion.1, f32[32,32]{0,1:T(8,128)S(1)} %maximum_maximum_fusion.2), channel_id=1, replica_groups=mesh['axial'=8,'trans'=32] {'axial','trans'}, use_global_device_ids=true, to_apply=%region_6.8 | all-reduce | flops 2048 | bytes 16384 | tf_op jit(solution)/shard_map/psum | solution.py:276
  269.6 2.9 cholesky.214
  273.9 2.4 custom-call.63
  276.9 2.9 cholesky.225
  281.2 2.4 custom-call.61
  284.2 1.5 cholesky.236
  287.0 1.2 custom-call.56
  288.9 1.5 cholesky.247
  291.7 1.2 custom-call.59
  293.7 1.5 cholesky.258
  296.5 1.2 custom-call.62
  304.0 3.0 collective-permute-start.14
  307.7 1.9 collective-permute-start.15
  310.3 4.4 collective-permute-done.15
  314.7 1.3 collective-permute-start.16
  316.1 1.5 collective-permute-start.17
  318.2 3.3 collective-permute-done.17
  321.9 2.1 copy.200
  324.0 3.9 copy.201
  328.0 12.2 %convolution_bitcast_fusion = f32[16,12,1,4,128]{1,0,4,3,2:T(8,128)} fusion(f32[16,48,4,128]{1,0,3,2:T(8,128)} %copy.201, f32[12,48,4,128]{1,0,3,2:T(8,128)} %copy.175), kind=kOutput, calls=%fused_computation.2 | convolution fusion | flops 56623104 | bytes 3145728 | tf_op jit(solution)/shard_map/abxyz,vbxyz->vaxyz/dot_general | solution.py:127
  340.2 3.2 copy.203
  346.3 3.1 collective-permute-start.18
  349.4 2.2 collective-permute-start.19
  353.3 3.1 collective-permute-done.19
  356.4 4.0 collective-permute-start.20
  360.4 1.3 collective-permute-start.21
  362.3 3.4 collective-permute-done.21
  370.2 81.9 %all-reduce.4 = (f32[48,48]{0,1:T(8,128)S(1)}, f32[48,48]{0,1:T(8,128)S(1)}) all-reduce(f32[48,48]{0,1:T(8,128)S(1)} %get-tuple-element.81, f32[48,48]{0,1:T(8,128)S(1)} %get-tuple-element.82), channel_id=1, replica_groups=mesh['axial'=8,'trans'=32] {'axial','trans'}, use_global_device_ids=true, to_apply=%region_10.16 | all-reduce | flops 4608 | bytes 36864 | tf_op jit(solution)/shard_map/psum | solution.py:276
  452.2 4.4 cholesky.269
  457.9 3.7 custom-call.73
  462.2 4.4 cholesky.280
  467.9 3.7 custom-call.71
  472.2 1.5 cholesky.291
  475.0 1.2 custom-call.66
  476.9 1.5 cholesky.302
  479.7 1.2 custom-call.69
  481.7 1.5 cholesky.313
  (266 shorter events, 61.8 us)
Async XLA Ops:
  0.6 15.4 %copy-start = (f32[16,3,2,8,128]{4,3,2,1,0:T(8,128)S(1)}, f32[16,3,2,8,128]{4,3,2,1,0:T(8,128)}, u32[]{:S(2)}) copy-start(f32[16,3,2,8,128]{4,3,2,1,0:T(8,128)} %param.21) | copy-start | bytes 1179652
  0.6 8.5 %copy-start.1 = (s32[2,8,128]{2,1,0:T(8,128)S(1)}, s32[2,8,128]{2,1,0:T(8,128)}, u32[]{:S(2)}) copy-start(s32[2,8,128]{2,1,0:T(8,128)} %param.22) | copy-start | bytes 24580
  0.7 8.5 %copy-start.3 = (f32[4]{0:T(128)S(1)}, f32[4]{0:T(128)}, u32[]{:S(2)}) copy-start(f32[4]{0:T(128)} %param.24) | copy-start | bytes 52
  0.7 8.5 %copy-start.2 = (f32[4]{0:T(128)S(1)}, f32[4]{0:T(128)}, u32[]{:S(2)}) copy-start(f32[4]{0:T(128)} %param.25) | copy-start | bytes 52
  2.6 14.4 %collective-permute-start.2 = (f32[16,3,1,8,128]{4,0,3,2,1:T(8,128)S(1)}, f32[16,3,1,8,128]{4,0,3,2,1:T(8,128)S(1)}, u32[]{:S(2)}, u32[]{:S(2)}) collective-permute-start(f32[16,3,1,8,128]{4,0,3,2,1:T(8,128)S(1)} %get-tuple-element.79), channel_id=1, source_target_pairs={{0,32},{32,64},{64,96},{96,128},{128,160},{160,192},{192,224},{1,3... | collective-permute-start | bytes 589832 | tf_op jit(solution)/shard_map/ppermute | solution.py:27
  7.1 9.9 %collective-permute-start.3 = (f32[16,3,1,8,128]{4,0,3,2,1:T(8,128)S(1)}, f32[16,3,1,8,128]{4,0,3,2,1:T(8,128)S(1)}, u32[]{:S(2)}, u32[]{:S(2)}) collective-permute-start(f32[16,3,1,8,128]{4,0,3,2,1:T(8,128)S(1)} %get-tuple-element.80), channel_id=1, source_target_pairs={{32,0},{64,32},{96,64},{128,96},{160,128},{192,160},{224,192},{33,... | collective-permute-start | bytes 589832 | tf_op jit(solution)/shard_map/ppermute | solution.py:28
  9.2 7.7 %collective-permute-start.1 = (f32[1,8,128]{2,1,0:T(8,128)S(1)}, f32[1,8,128]{2,1,0:T(8,128)S(1)}, u32[]{:S(2)}, u32[]{:S(2)}) collective-permute-start(f32[1,8,128]{2,1,0:T(8,128)S(1)} %slice.722), channel_id=1, source_target_pairs={{0,32},{32,64},{64,96},{96,128},{128,160},{160,192},{192,224},{1,3... | collective-permute-start | bytes 12296 | tf_op jit(solution)/shard_map/ppermute | solution.py:17
  12.8 4.1 collective-permute-start
  17.0 5.7 %collective-permute-start.4 = (f32[16,3,4,1,128]{4,0,3,2,1:T(8,128)S(1)}, f32[16,3,4,1,128]{4,0,3,2,1:T(8,128)S(1)}, u32[]{:S(2)}, u32[]{:S(2)}) collective-permute-start(f32[16,3,4,1,128]{4,0,3,2,1:T(8,128)S(1)} %get-tuple-element.65), channel_id=1, source_target_pairs={{0,1},{1,2},{2,3},{3,4},{4,5},{5,6},{6,7},{7,8},{8,9},{9,10},{10,1... | collective-permute-start | bytes 294920 | tf_op jit(solution)/shard_map/ppermute | solution.py:27
  20.5 6.1 %collective-permute-start.5 = (f32[16,3,4,1,128]{4,0,3,2,1:T(8,128)S(1)}, f32[16,3,4,1,128]{4,0,3,2,1:T(8,128)S(1)}, u32[]{:S(2)}, u32[]{:S(2)}) collective-permute-start(f32[16,3,4,1,128]{4,0,3,2,1:T(8,128)S(1)} %get-tuple-element.66), channel_id=1, source_target_pairs={{1,0},{2,1},{3,2},{4,3},{5,4},{6,5},{7,6},{8,7},{9,8},{10,9},{11,1... | collective-permute-start | bytes 294920 | tf_op jit(solution)/shard_map/ppermute | solution.py:28
  120.9 9.1 %collective-permute-start.6 = (f32[16,3,1,8,128]{4,0,3,1,2:T(8,128)S(1)}, f32[16,3,1,8,128]{4,0,3,1,2:T(8,128)S(1)}, u32[]{:S(2)}, u32[]{:S(2)}) collective-permute-start(f32[16,3,1,8,128]{4,0,3,1,2:T(8,128)S(1)} %copy.293), channel_id=1, source_target_pairs={{0,32},{32,64},{64,96},{96,128},{128,160},{160,192},{192,224},{1,3... | collective-permute-start | bytes 589832 | tf_op jit(solution)/shard_map/ppermute | solution.py:27
  127.4 7.0 %collective-permute-start.7 = (f32[16,3,1,8,128]{4,0,3,1,2:T(8,128)S(1)}, f32[16,3,1,8,128]{4,0,3,1,2:T(8,128)S(1)}, u32[]{:S(2)}, u32[]{:S(2)}) collective-permute-start(f32[16,3,1,8,128]{4,0,3,1,2:T(8,128)S(1)} %copy.294), channel_id=1, source_target_pairs={{32,0},{64,32},{96,64},{128,96},{160,128},{192,160},{224,192},{33,... | collective-permute-start | bytes 589832 | tf_op jit(solution)/shard_map/ppermute | solution.py:28
  134.4 4.0 collective-permute-start.8
  136.0 5.4 %collective-permute-start.9 = (f32[16,3,4,1,128]{4,0,3,1,2:T(8,128)S(1)}, f32[16,3,4,1,128]{4,0,3,1,2:T(8,128)S(1)}, u32[]{:S(2)}, u32[]{:S(2)}) collective-permute-start(f32[16,3,4,1,128]{4,0,3,1,2:T(8,128)S(1)} %get-tuple-element.64), channel_id=1, source_target_pairs={{1,0},{2,1},{3,2},{4,3},{5,4},{6,5},{7,6},{8,7},{9,8},{10,9},{11,1... | collective-permute-start | bytes 294920 | tf_op jit(solution)/shard_map/ppermute | solution.py:28
  164.7 6.8 %collective-permute-start.10 = (f32[16,3,1,8,128]{4,0,3,2,1:T(8,128)S(1)}, f32[16,3,1,8,128]{4,0,3,2,1:T(8,128)S(1)}, u32[]{:S(2)}, u32[]{:S(2)}) collective-permute-start(f32[16,3,1,8,128]{4,0,3,2,1:T(8,128)S(1)} %get-tuple-element.75), channel_id=1, source_target_pairs={{0,32},{32,64},{64,96},{96,128},{128,160},{160,192},{192,224},{1,3... | collective-permute-start | bytes 589832 | tf_op jit(solution)/shard_map/ppermute | solution.py:27
  168.1 7.0 %collective-permute-start.11 = (f32[16,3,1,8,128]{4,0,3,2,1:T(8,128)S(1)}, f32[16,3,1,8,128]{4,0,3,2,1:T(8,128)S(1)}, u32[]{:S(2)}, u32[]{:S(2)}) collective-permute-start(f32[16,3,1,8,128]{4,0,3,2,1:T(8,128)S(1)} %get-tuple-element.76), channel_id=1, source_target_pairs={{32,0},{64,32},{96,64},{128,96},{160,128},{192,160},{224,192},{33,... | collective-permute-start | bytes 589832 | tf_op jit(solution)/shard_map/ppermute | solution.py:28
  175.2 5.1 %collective-permute-start.12 = (f32[16,3,4,1,128]{4,0,3,2,1:T(8,128)S(1)}, f32[16,3,4,1,128]{4,0,3,2,1:T(8,128)S(1)}, u32[]{:S(2)}, u32[]{:S(2)}) collective-permute-start(f32[16,3,4,1,128]{4,0,3,2,1:T(8,128)S(1)} %get-tuple-element.61), channel_id=1, source_target_pairs={{0,1},{1,2},{2,3},{3,4},{4,5},{5,6},{6,7},{7,8},{8,9},{9,10},{10,1... | collective-permute-start | bytes 294920 | tf_op jit(solution)/shard_map/ppermute | solution.py:27
  178.7 5.4 %collective-permute-start.13 = (f32[16,3,4,1,128]{4,0,3,2,1:T(8,128)S(1)}, f32[16,3,4,1,128]{4,0,3,2,1:T(8,128)S(1)}, u32[]{:S(2)}, u32[]{:S(2)}) collective-permute-start(f32[16,3,4,1,128]{4,0,3,2,1:T(8,128)S(1)} %get-tuple-element.62), channel_id=1, source_target_pairs={{1,0},{2,1},{3,2},{4,3},{5,4},{6,5},{7,6},{8,7},{9,8},{10,9},{11,1... | collective-permute-start | bytes 294920 | tf_op jit(solution)/shard_map/ppermute | solution.py:28
  304.0 6.2 %collective-permute-start.14 = (f32[16,3,1,8,128]{4,0,3,1,2:T(8,128)S(1)}, f32[16,3,1,8,128]{4,0,3,1,2:T(8,128)S(1)}, u32[]{:S(2)}, u32[]{:S(2)}) collective-permute-start(f32[16,3,1,8,128]{4,0,3,1,2:T(8,128)S(1)} %copy.295), channel_id=1, source_target_pairs={{0,32},{32,64},{64,96},{96,128},{128,160},{160,192},{192,224},{1,3... | collective-permute-start | bytes 589832 | tf_op jit(solution)/shard_map/ppermute | solution.py:27
  307.7 7.0 %collective-permute-start.15 = (f32[16,3,1,8,128]{4,0,3,1,2:T(8,128)S(1)}, f32[16,3,1,8,128]{4,0,3,1,2:T(8,128)S(1)}, u32[]{:S(2)}, u32[]{:S(2)}) collective-permute-start(f32[16,3,1,8,128]{4,0,3,1,2:T(8,128)S(1)} %copy.296), channel_id=1, source_target_pairs={{32,0},{64,32},{96,64},{128,96},{160,128},{192,160},{224,192},{33,... | collective-permute-start | bytes 589832 | tf_op jit(solution)/shard_map/ppermute | solution.py:28
  314.7 3.5 collective-permute-start.16
  316.1 5.5 %collective-permute-start.17 = (f32[16,3,4,1,128]{4,0,3,1,2:T(8,128)S(1)}, f32[16,3,4,1,128]{4,0,3,1,2:T(8,128)S(1)}, u32[]{:S(2)}, u32[]{:S(2)}) collective-permute-start(f32[16,3,4,1,128]{4,0,3,1,2:T(8,128)S(1)} %get-tuple-element.60), channel_id=1, source_target_pairs={{1,0},{2,1},{3,2},{4,3},{5,4},{6,5},{7,6},{8,7},{9,8},{10,9},{11,1... | collective-permute-start | bytes 294920 | tf_op jit(solution)/shard_map/ppermute | solution.py:28
  346.3 7.0 %collective-permute-start.18 = (f32[16,3,1,8,128]{4,0,3,2,1:T(8,128)S(1)}, f32[16,3,1,8,128]{4,0,3,2,1:T(8,128)S(1)}, u32[]{:S(2)}, u32[]{:S(2)}) collective-permute-start(f32[16,3,1,8,128]{4,0,3,2,1:T(8,128)S(1)} %get-tuple-element.71), channel_id=1, source_target_pairs={{0,32},{32,64},{64,96},{96,128},{128,160},{160,192},{192,224},{1,3... | collective-permute-start | bytes 589832 | tf_op jit(solution)/shard_map/ppermute | solution.py:27
  349.4 7.0 %collective-permute-start.19 = (f32[16,3,1,8,128]{4,0,3,2,1:T(8,128)S(1)}, f32[16,3,1,8,128]{4,0,3,2,1:T(8,128)S(1)}, u32[]{:S(2)}, u32[]{:S(2)}) collective-permute-start(f32[16,3,1,8,128]{4,0,3,2,1:T(8,128)S(1)} %get-tuple-element.72), channel_id=1, source_target_pairs={{32,0},{64,32},{96,64},{128,96},{160,128},{192,160},{224,192},{33,... | collective-permute-start | bytes 589832 | tf_op jit(solution)/shard_map/ppermute | solution.py:28
  356.4 5.9 %collective-permute-start.20 = (f32[16,3,4,1,128]{4,0,3,2,1:T(8,128)S(1)}, f32[16,3,4,1,128]{4,0,3,2,1:T(8,128)S(1)}, u32[]{:S(2)}, u32[]{:S(2)}) collective-permute-start(f32[16,3,4,1,128]{4,0,3,2,1:T(8,128)S(1)} %get-tuple-element.57), channel_id=1, source_target_pairs={{0,1},{1,2},{2,3},{3,4},{4,5},{5,6},{6,7},{7,8},{8,9},{9,10},{10,1... | collective-permute-start | bytes 294920 | tf_op jit(solution)/shard_map/ppermute | solution.py:27
  360.4 5.4 %collective-permute-start.21 = (f32[16,3,4,1,128]{4,0,3,2,1:T(8,128)S(1)}, f32[16,3,4,1,128]{4,0,3,2,1:T(8,128)S(1)}, u32[]{:S(2)}, u32[]{:S(2)}) collective-permute-start(f32[16,3,4,1,128]{4,0,3,2,1:T(8,128)S(1)} %get-tuple-element.58), channel_id=1, source_target_pairs={{1,0},{2,1},{3,2},{4,3},{5,4},{6,5},{7,6},{8,7},{9,8},{10,9},{11,1... | collective-permute-start | bytes 294920 | tf_op jit(solution)/shard_map/ppermute | solution.py:28
where the time goes:
time: 499 us; the launch traced here: 492 us
  blocking collectives  249 us (50%)
  other arithmetic  69.1 us (14%)
  matrix products  55.9 us (11%)
  starting transfers between devices  54.6 us (11%)
  waiting for transfers between devices  33.8 us (7%)
  local copies, waits for them, and re-layouts  27.1 us (5%)
    psum x2, blocking collectives, on_device(): lax.psum(mass_terms(blocks, permittivity_cell), ('axial', 'trans'))  164 us
    psum x1, blocking collectives, on_device(): lax.psum((mass_terms([mode_block], permittivity_cell), stiff_terms([mode_...  85.4 us
    ppermute x10, waiting for transfers between devices, extended(): after = lax.ppermute(first, axis, down)  32.8 us
    ppermute x10, starting transfers between devices, extended(): before = lax.ppermute(last, axis, up)  30.6 us
    dot_general x2, matrix products, block_solve(): jnp.einsum('abxyz,vbxyz->vaxyz', block_inverse, patches, precision=highest)  24.4 us
    ppermute x10, starting transfers between devices, extended(): after = lax.ppermute(first, axis, down)  17.2 us
    another operation x18, other arithmetic, rayleigh_ritz(): jnp.linalg.cholesky(jnp.dot(subspace.T, subspace, precision=highest))  12.9 us
    another operation x4, local copies, waits for them, and re-layouts  11.6 us
  transfers between devices with their start and end apart: 22, of which 11 were waited for; matrix products, arithmetic and copies ran while one was open for 2% of the time, Pallas kernels for 0%

commit v1 on v0

v1 whole, which is shorter than its diff:
```python
import functools
import itertools
import jax
import jax.numpy as jnp
from jax import lax
from jax.experimental import pallas as pl
from jax.experimental.pallas import tpu as pltpu
from jax.sharding import PartitionSpec as P

V = 16
INNER = 3
MESH = pl.DeviceIdType.MESH
highest = lax.Precision.HIGHEST
NBRS = [(dx, dy) for dx in (-1, 0, 1) for dy in (-1, 0, 1) if (dx, dy) != (0, 0)]
SX, SY, SZ = 2, 8, 128
BASE = 64
f32 = jnp.float32


def nn(a, b):
    return lax.dot_general(a, b, (((1,), (0,)), ((), ())), precision=highest, preferred_element_type=f32)


def nt(a, b):
    return lax.dot_general(a, b, (((1,), (1,)), ((), ())), precision=highest, preferred_element_type=f32)


def tn(a, b):
    return lax.dot_general(a, b, (((0,), (0,)), ((), ())), precision=highest, preferred_element_type=f32)


def lanes_of(shape):
    return lax.broadcasted_iota(jnp.int32, shape, len(shape) - 1)


def rows_of(shape):
    return lax.broadcasted_iota(jnp.int32, shape, len(shape) - 2)


def shift_up(v):
    return jnp.where(lanes_of(v.shape) == SZ - 1, 0.0, pltpu.roll(v, SZ - 1, v.ndim - 1))


def shift_down(v):
    return jnp.where(lanes_of(v.shape) == 0, 0.0, pltpu.roll(v, 1, v.ndim - 1))


def place(base):
    shape = (V, 128)
    return (lanes_of(shape) == rows_of(shape) + base).astype(f32)


def eliminate(aug, full):
    shape = aug.shape
    row_at = rows_of(shape)
    for j in range(V):
        row = jnp.broadcast_to(aug[j : j + 1, :], shape)
        col = jnp.broadcast_to(aug[:, BASE + j : BASE + j + 1], shape)
        pivot = jnp.broadcast_to(aug[j : j + 1, BASE + j : BASE + j + 1], shape)
        factor = jnp.where((row_at != j) if full else (row_at > j), col / pivot, 0.0)
        aug = aug - factor * row
    diag = jnp.sum(jnp.where(lanes_of(shape) == row_at + BASE, aug, 0.0), axis=1, keepdims=True)
    return aug, jnp.broadcast_to(diag, shape)


def low_lanes(a, count):
    return jnp.where(lanes_of(a.shape) < count, a, 0.0)


def pad_rows(a, before, total):
    parts = []
    if before:
        parts.append(jnp.zeros((before, 128), f32))
    parts.append(a)
    after = total - before - a.shape[0]
    if after:
        parts.append(jnp.zeros((after, 128), f32))
    return jnp.concatenate(parts, axis=0) if len(parts) > 1 else a


def solve_start(packed):
    swept, diag = eliminate(packed, True)
    ratio = low_lanes(swept / diag, V)
    stiff = low_lanes(packed, V)
    mass = low_lanes(pltpu.roll(packed, 128 - BASE, 1), V)
    swept2, diag2 = eliminate(pltpu.roll(stiff, BASE, 1) + place(0), True)
    inverse = low_lanes(swept2 / diag2, V)
    return ratio, inverse, stiff, mass


def project(work, packed, known, inv_known, stiff_known, mass_known, start):
    total = known + V
    stiff_row = low_lanes(packed, total)
    mass_row = low_lanes(pltpu.roll(packed, 128 - BASE, 1), total)
    spot = place(known)
    lanes = lanes_of((V, 128))
    pad = 128 - known

    def square(known_part, row):
        corner = jnp.where(lanes < known, row, 0.0)
        top = known_part + tn(corner, spot)[:known]
        return pad_rows(jnp.concatenate([top, row], axis=0), 0, 128)

    stiff = square(stiff_known, stiff_row)
    mass = square(mass_known, mass_row)
    inv_pad = pad_rows(inv_known, 0, 128)
    coupling = jnp.where(lanes < known, stiff_row, 0.0)
    reach = nn(coupling, inv_pad)
    own = jnp.where((lanes >= known) & (lanes < total), stiff_row, 0.0)
    own = pltpu.roll(own, (BASE - known) % 128, 1)
    schur = own - nt(reach, pad_rows(coupling, BASE, 128))
    joint = spot - reach
    swept, diag = eliminate(schur + joint, True)
    solved = low_lanes(swept / diag, total)
    inverse = inv_pad + tn(joint, solved)
    step = nn(mass, inverse)
    coeffs = start
    for repeat in range(INNER):
        coeffs = nn(coeffs, step)
        weighted = nn(coeffs, mass)
        work[...] = nt(weighted, pad_rows(coeffs, BASE, 128))
        swept, diag = eliminate(work[...] + coeffs, False)
        coeffs = low_lanes(swept / jnp.sqrt(diag), total)
    rayleigh = nt(nn(coeffs, stiff), pad_rows(coeffs, 0, 128))
    return coeffs, rayleigh, inverse, stiff, mass


def kernel(
    geo,
    x0_ref,
    region_ref,
    mask_ref,
    nu_tab,
    eps_tab,
    binv_any,
    modes_ref,
    resid_ref,
    fx,
    fax,
    fw1,
    faw1,
    fw2,
    faw2,
    fr,
    flux,
    mat,
    keep,
    nub,
    epsb,
    binv,
    part,
    work,
    *rest,
):
    stage_sets, sizes, dims = geo
    n_stage = len(stage_sets)
    bufs = rest[: 3 * n_stage]
    (halo_send, halo_recv, red_send, red_recv, binv_sem) = rest[3 * n_stage :]
    n_axial, n_trans = dims
    a_me, t_me = lax.axis_index("axial"), lax.axis_index("trans")
    me = {"x": a_me // 2, "c": a_me % 2, "z": t_me // sizes["y"], "y": t_me % sizes["y"]}

    binv_copy = pltpu.make_async_copy(binv_any, binv, binv_sem)
    binv_copy.start()

    def moved(offset):
        spot = dict(me)
        for d in offset:
            spot[d] = lax.rem(me[d] + offset[d], sizes[d])
        return (spot["x"] * 2 + spot["c"], spot["z"] * sizes["y"] + spot["y"])

    def neighbour(dx, dy):
        return (lax.rem(a_me + dx + n_axial, n_axial), lax.rem(t_me + dy + n_trans, n_trans))

    def offsets(stage):
        return [
            dict(zip(stage, o)) for o in itertools.product(*[range(sizes[d]) for d in stage]) if any(o)
        ]

    def rank(stage):
        r = 0
        for d in stage:
            r = r * sizes[d] + me[d]
        return r

    barrier = pltpu.get_barrier_semaphore()
    greeted = 0
    for dx, dy in NBRS:
        pl.semaphore_signal(barrier, inc=1, device_id=neighbour(dx, dy), device_id_type=MESH)
        greeted += 1
    for stage in stage_sets:
        for o in offsets(stage):
            pl.semaphore_signal(barrier, inc=1, device_id=moved(o), device_id_type=MESH)
            greeted += 1

    region = region_ref[...]
    nu = jnp.zeros(region.shape, f32)
    eps = jnp.zeros(region.shape, f32)
    for level in range(4):
        here = region == level
        nu = jnp.where(here, nu_tab[level], nu)
        eps = jnp.where(here, eps_tab[level], eps)
    keep_f = mask_ref[...].astype(f32)
    for x in range(SX):
        for y in range(SY):
            mat[1 + x, 1 + y, 0:1, :] = nu[x, y : y + 1, :]
            mat[1 + x, 1 + y, 1:2, :] = eps[x, y : y + 1, :]
            for c in range(3):
                row = keep_f[c, x, y : y + 1, :]
                keep[x, y, c] = jnp.broadcast_to(row, (V, SZ))
                field = x0_ref[pl.ds(c * SX * SY + x * SY + y, V, stride=3 * SX * SY), :]
                fx[1 + x, 1 + y, c] = field * row

    pl.semaphore_wait(barrier, greeted)

    def halo_start(ref, which):
        copies = []
        for k, (dx, dy) in enumerate(NBRS):
            sx = pl.ds(1, SX) if dx == 0 else pl.ds(1 if dx < 0 else SX, 1)
            tx = pl.ds(1, SX) if dx == 0 else pl.ds(SX + 1 if dx < 0 else 0, 1)
            sy = pl.ds(1, SY) if dy == 0 else pl.ds(1 if dy < 0 else SY, 1)
            ty = pl.ds(1, SY) if dy == 0 else pl.ds(SY + 1 if dy < 0 else 0, 1)
            copy = pltpu.make_async_remote_copy(
                src_ref=ref.at[sx, sy],
                dst_ref=ref.at[tx, ty],
                send_sem=halo_send.at[which, k],
                recv_sem=halo_recv.at[which, k],
                device_id=neighbour(dx, dy),
                device_id_type=MESH,
            )
            copy.start()
            copies.append(copy)
        return copies

    def halo_finish(ref, copies):
        for copy in copies:
            copy.wait_recv()

        @pl.when(a_me == 0)
        def _():
            ref[0] = jnp.zeros(ref.shape[1:], f32)

        @pl.when(a_me == n_axial - 1)
        def _():
            ref[SX + 1] = jnp.zeros(ref.shape[1:], f32)

        @pl.when(t_me == 0)
        def _():
            ref[:, 0] = jnp.zeros((ref.shape[0],) + ref.shape[2:], f32)

        @pl.when(t_me == n_trans - 1)
        def _():
            ref[:, SY + 1] = jnp.zeros((ref.shape[0],) + ref.shape[2:], f32)

        for copy in copies:
            copy.wait_send()

    def reduce_stage(value, phase, s):
        stage = stage_sets[s]
        buf = bufs[phase * n_stage + s]
        r = rank(stage)
        buf[r] = value
        copies = []
        base = sum(len(offsets(st)) for st in stage_sets[:s])
        for k, o in enumerate(offsets(stage)):
            copy = pltpu.make_async_remote_copy(
                src_ref=buf.at[r],
                dst_ref=buf.at[r],
                send_sem=red_send.at[phase, base + k],
                recv_sem=red_recv.at[phase, base + k],
                device_id=moved(o),
                device_id_type=MESH,
            )
            copy.start()
            copies.append(copy)
        return buf, copies

    def reduce_finish(buf, copies):
        for copy in copies:
            copy.wait_recv()
        value = buf[0]
        for k in range(1, len(copies) + 1):
            value = value + buf[k]
        for copy in copies:
            copy.wait_send()
        return value

    def reduce_all(value, phase, halo):
        for s in range(n_stage):
            buf, copies = reduce_stage(value, phase, s)
            value = reduce_finish(buf, copies)
            if s == 0 and halo is not None:
                halo_copies = halo_start(halo[0], halo[1])
        if halo is not None:
            halo_finish(halo[0], halo_copies)
        return value

    def operate(src, dst):
        for x in range(SX + 1):
            here = lambda c, ox, oy: src[x + ox, pl.ds(oy, SY + 1), c]
            weight = nub[x]
            ex, ey, ez = here(0, 0, 0), here(1, 0, 0), here(2, 0, 0)
            flux[x, :, 0] = weight * (here(2, 0, 1) - ez - shift_up(ey) + ey)
            flux[x, :, 1] = weight * (shift_up(ex) - ex - here(2, 1, 0) + ez)
            flux[x, :, 2] = weight * (here(1, 1, 0) - ey - here(0, 0, 1) + ex)
            zz = here(2, 1, 1)
            flux[x, :, 3] = (
                here(0, 1, 1) - here(0, 0, 1) + here(1, 1, 1) - here(1, 1, 0) + zz - shift_down(zz)
            )
        for x in range(SX):
            hx = lambda oy: flux[x + 1, pl.ds(oy, SY), 0]
            hy = lambda ox: flux[x + ox, pl.ds(1, SY), 1]
            hz = lambda ox, oy: flux[x + ox, pl.ds(oy, SY), 2]
            q = lambda ox, oy: flux[x + ox, pl.ds(oy, SY), 3]
            hx1, hy1, hz1, q0 = hx(1), hy(1), hz(1, 1), q(0, 0)
            last = lanes_of(q0.shape) == SZ - 1
            above = jnp.where(last, -src[x + 1, pl.ds(1, SY), 2], pltpu.roll(q0, SZ - 1, q0.ndim - 1))
            dst[x + 1, pl.ds(1, SY), 0] = keep[x, :, 0] * (
                hz1 - hz(1, 0) - hy1 + shift_down(hy1) + q0 - q(1, 0)
            )
            dst[x + 1, pl.ds(1, SY), 1] = keep[x, :, 1] * (
                hx1 - shift_down(hx1) - hz1 + hz(0, 1) + q0 - q(0, 1)
            )
            dst[x + 1, pl.ds(1, SY), 2] = keep[x, :, 2] * (
                hy1 - hy(0) - hx1 + hx(0) + q0 - above
            )

    def gram(fields, image, newest):
        count = V * len(fields)
        part[...] = jnp.zeros(part.shape, f32)

        def body(y, carry):
            left, right = [], []
            for x in range(SX):
                e = jnp.broadcast_to(epsb[x + 1, y + 1][0:1], (V, SZ))
                for c in range(3):
                    w = newest[x + 1, y + 1, c]
                    left.append(jnp.concatenate([image[x + 1, y + 1, c], w * e], axis=0))
                    right.append(jnp.concatenate([f[x + 1, y + 1, c] for f in fields], axis=0))
            part[:, 0:count] += nt(jnp.concatenate(left, axis=1), jnp.concatenate(right, axis=1))
            return carry

        lax.fori_loop(0, SY, body, 0)
        both = part[...]
        return both[0:V] + pltpu.roll(both[V : 2 * V], BASE, 1)

    def residual(rows, images, fields, rows_mass, y_range, x_range, store):
        coeffs = jnp.concatenate([rows, -rows_mass], axis=1)

        def body(y, carry):
            pieces = []
            for x in x_range:
                e = jnp.broadcast_to(epsb[x, y][0:1], (V, SZ))
                for c in range(3):
                    pieces.append(
                        jnp.concatenate(
                            [f[x, y, c] for f in images] + [f[x, y, c] * e for f in fields], axis=0
                        )
                    )
            out = nn(coeffs, jnp.concatenate(pieces, axis=1))
            k = 0
            for x in x_range:
                for c in range(3):
                    store(x, y, c, out[:, k * SZ : (k + 1) * SZ])
                    k += 1
            return carry

        lax.fori_loop(*y_range, body, 0)

    def store_r(x, y, c, value):
        fr[x, y, c] = value

    def precondition(dst):
        for yb in range(SY // 2):
            acc = jnp.zeros((12, V, SZ), f32)

            def body(i, acc):
                c2 = i // 4
                ox = i - 4 * c2
                for oy in range(4):
                    patch = fr[ox, 2 * yb + oy, c2]
                    rows = [
                        binv[pl.ds(a * 192 + i * 16 + oy * 4 + yb, 1), :] for a in range(12)
                    ]
                    acc = acc + jnp.stack([jnp.broadcast_to(r, (V, SZ)) * patch for r in rows])
                return acc

            acc = lax.fori_loop(0, 12, body, acc)
            for c in range(3):
                for cx in range(2):
                    for cy in range(2):
                        dst[1 + cx, 1 + 2 * yb + cy, c] = (
                            keep[cx, 2 * yb + cy, c] * acc[4 * c + 2 * cx + cy]
                        )

    mat_copies = halo_start(mat, 0)
    x_copies = halo_start(fx, 1)
    halo_finish(mat, mat_copies)
    for x in range(SX + 2):
        for y in range(SY + 2):
            if x <= SX and y <= SY:
                nub[x, y] = jnp.broadcast_to(mat[x, y, 0:1, :], (V, SZ))
            epsb[x, y] = jnp.broadcast_to(mat[x, y, 1:2, :], (8, SZ))
    halo_finish(fx, x_copies)

    scale = 1.0 / (SX * SY * SZ * n_axial * n_trans)
    operate(fx, fax)
    packed = reduce_all(gram([fx], fax, fx), 0, (fax, 2)) * scale
    ratio, inverse, stiff, mass = solve_start(packed)
    rows_mass = tn(ratio, place(0))[0:V, 0:V]
    binv_copy.wait()
    residual(place(0)[:, 0:V], [fax], [fx], rows_mass, (0, SY + 2), range(SX + 2), store_r)
    precondition(fw1)
    halo_finish(fw1, halo_start(fw1, 3))
    operate(fw1, faw1)
    packed = reduce_all(gram([fx, fw1], faw1, fw1), 1, (faw1, 4)) * scale
    coeffs, rayleigh, inverse, stiff, mass = project(work, packed, V, inverse, stiff, mass, place(0))
    weighted = nn(low_lanes(rayleigh, V), pad_rows(coeffs, 0, 128))
    residual(
        coeffs[:, 0 : 2 * V], [fax, faw1], [fx, fw1], weighted[:, 0 : 2 * V], (0, SY + 2), range(SX + 2), store_r
    )
    precondition(fw2)
    halo_finish(fw2, halo_start(fw2, 5))
    operate(fw2, faw2)
    packed = reduce_all(gram([fx, fw1, fw2], faw2, fw2), 2, None) * scale
    coeffs, rayleigh, _, _, _ = project(
        work, packed, 2 * V, inverse[0 : 2 * V], stiff[0 : 2 * V], mass[0 : 2 * V], coeffs
    )
    weighted = nn(low_lanes(rayleigh, V), pad_rows(coeffs, 0, 128))

    def rows_at(c, x, y):
        return pl.ds(c * SX * SY + (x - 1) * SY + (y - 1), V, stride=3 * SX * SY)

    def store_out(x, y, c, value):
        resid_ref[rows_at(c, x, y), :] = value

    core_x = range(1, SX + 1)
    residual(
        coeffs[:, 0 : 3 * V],
        [fax, faw1, faw2],
        [fx, fw1, fw2],
        weighted[:, 0 : 3 * V],
        (1, SY + 1),
        core_x,
        store_out,
    )

    def body(y, carry):
        pieces = []
        for x in core_x:
            for c in range(3):
                pieces.append(jnp.concatenate([f[x, y, c] for f in (fx, fw1, fw2)], axis=0))
        out = nn(coeffs[:, 0 : 3 * V], jnp.concatenate(pieces, axis=1))
        k = 0
        for x in core_x:
            for c in range(3):
                modes_ref[rows_at(c, x, y), :] = out[:, k * SZ : (k + 1) * SZ]
                k += 1
        return carry

    lax.fori_loop(1, SY + 1, body, 0)


def on_device(geo, start_modes, region, edge_mask, reluctivity, permittivity, block_inverse):
    stage_sets, sizes, dims = geo
    ext = pltpu.VMEM((SX + 2, SY + 2, 3, V, SZ), f32)
    members = []
    for stage in stage_sets:
        n = 1
        for d in stage:
            n *= sizes[d]
        members.append(n)
    messages = sum(n - 1 for n in members)
    vmem = pl.BlockSpec(memory_space=pltpu.VMEM)
    smem = pl.BlockSpec(memory_space=pltpu.SMEM)
    modes, resid = pl.pallas_call(
        functools.partial(kernel, geo),
        out_shape=[jax.ShapeDtypeStruct((V * 3 * SX * SY, SZ), f32)] * 2,
        in_specs=[vmem, vmem, vmem, smem, smem, pl.BlockSpec(memory_space=pl.ANY)],
        out_specs=[vmem, vmem],
        scratch_shapes=[ext] * 7
        + [
            pltpu.VMEM((SX + 1, SY + 1, 4, V, SZ), f32),
            pltpu.VMEM((SX + 2, SY + 2, 8, SZ), f32),
            pltpu.VMEM((SX, SY, 3, V, SZ), f32),
            pltpu.VMEM((SX + 1, SY + 1, V, SZ), f32),
            pltpu.VMEM((SX + 2, SY + 2, 8, SZ), f32),
            pltpu.VMEM((12 * 48 * SY // 2, SZ), f32),
            pltpu.VMEM((2 * V, SZ), f32),
            pltpu.VMEM((V, 128), f32),
        ]
        + [pltpu.VMEM((n, V, SZ), f32) for _ in range(3) for n in members]
        + [
            pltpu.SemaphoreType.DMA((6, 8)),
            pltpu.SemaphoreType.DMA((6, 8)),
            pltpu.SemaphoreType.DMA((3, messages)),
            pltpu.SemaphoreType.DMA((3, messages)),
            pltpu.SemaphoreType.DMA,
        ],
        compiler_params=pltpu.CompilerParams(
            collective_id=0, has_side_effects=True, vmem_limit_bytes=48 * 1024 * 1024
        ),
        name="cavity",
    )(
        start_modes.reshape(V * 3 * SX * SY, SZ),
        region,
        edge_mask,
        reluctivity,
        permittivity,
        block_inverse.reshape(12 * 48 * SY // 2, SZ),
    )
    shape = (V, 3, SX, SY, SZ)
    return modes.reshape(shape), resid.reshape(shape)


def geometry(mesh):
    n_axial, n_trans = mesh.shape["axial"], mesh.shape["trans"]
    y = 4 if n_trans % 16 == 0 else 2
    sizes = {"c": 2, "x": n_axial // 2, "z": n_trans // y, "y": y}
    return (("c", "z"), ("x", "y")), sizes, (n_axial, n_trans)


def solution(mesh):
    in_specs = (
        P(None, None, "axial", "trans", None),
        P("axial", "trans", None),
        P(None, "axial", "trans", None),
        P(),
        P(),
        P(None, None, "axial", "trans", None),
    )
    out_specs = (P(None, None, "axial", "trans", None), P(None, None, "axial", "trans", None))
    return jax.shard_map(
        functools.partial(on_device, geometry(mesh)),
        mesh=mesh,
        in_specs=in_specs,
        out_specs=out_specs,
        check_vma=False,
    )
```

time: 499 us -> 122 us (0.24); the launches traced: 492 us -> 121 us
  blocking collectives: 249 us -> 0 us
  Pallas kernels: 0 us -> 114 us
  other arithmetic: 69.1 us -> 0 us
  matrix products: 55.9 us -> 0 us
  starting transfers between devices: 54.6 us -> 0 us
  waiting for transfers between devices: 33.8 us -> 0 us
  local copies, waits for them, and re-layouts: 27.1 us -> 6.5 us
    psum x3 -> x0, blocking collectives: 249 us -> none  [the longest x2 164 us: on_device(): lax.psum(mass_terms(blocks, permittivity_cell), ('axial', 'trans'))]
    pallas_call x0 -> x1, Pallas kernels: none -> 114 us  [on_device(): pl.pallas_call(functools.partial(kernel, geo), out_shape=[jax.ShapeDtypeS...]
    another operation x60 -> x0, other arithmetic: 61.5 us -> none  [the longest x18 12.9 us: rayleigh_ritz(): jnp.linalg.cholesky(jnp.dot(subspace.T, subspace, precision=highest))]
    ppermute x22 -> x0, starting transfers between devices: 54.6 us -> none  [the longest x10 30.6 us: extended(): before = lax.ppermute(last, axis, up)]
    dot_general x57 -> x0, matrix products: 51.6 us -> none  [the longest x2 24.4 us: block_solve(): jnp.einsum('abxyz,vbxyz->vaxyz', block_inverse, patches, precision=highest)]
    ppermute x22 -> x0, waiting for transfers between devices: 33.8 us -> none  [the longest x10 32.8 us: extended(): after = lax.ppermute(first, axis, down)]
    another operation x10 -> x0, local copies, waits for them, and re-layouts: 16.1 us -> none
    transpose x4 -> x0, local copies, waits for them, and re-layouts: 6.54 us -> none  [the longest x2 6.47 us: block_solve(): jnp.einsum('abxyz,vbxyz->vaxyz', block_inverse, patches, precision=highest)]
  transfers between devices with their start and end apart: 22 -> 0, of which waited for: 11 -> 0; matrix products, arithmetic and copies ran while one was open for 2% -> 0% of each run, Pallas kernels for 0% -> 0%
where the time goes in v1:
time: 122 us; the launch traced here: 121 us
  Pallas kernels  114 us (93%)
  local copies, waits for them, and re-layouts  6.5 us (5%)
    pallas_call x1, Pallas kernels, on_device(): pl.pallas_call(functools.partial(kernel, geo), out_shape=[jax.ShapeDtypeS...  114 us
    unnamed x14, local copies, waits for them, and re-layouts  6.5 us

profile of v1, /device:TPU:1, one launch (start us, length us, event | category | flops | bytes accessed | tf_op | source)
XLA Modules:
  0.0 121.3 jit_solution(1118939340057666243)
XLA Ops:
  0.6 0.0 copy-start
  0.6 1.3 %copy-done = f32[12,48,1,4,128]{4,3,2,1,0:T(4,128)S(1)} copy-done((f32[12,48,1,4,128]{4,3,2,1,0:T(4,128)S(1)}, f32[12,48,1,4,128]{4,3,2,1,0:T(4,128)}, u32[]{:S(2)}) %copy-start) | copy-done | bytes 1179672
  1.9 0.0 copy-start.1
  1.9 1.0 copy-done.1
  2.9 0.0 copy-start.2
  2.9 0.7 copy-done.2
  3.6 0.0 copy-start.3
  3.6 0.7 copy-done.3
  4.3 0.0 copy-start.4
  4.3 0.7 copy-done.4
  5.0 0.0 copy-start.5
  5.0 0.7 copy-done.5
  5.6 114.1 %cavity.1 = (f32[768,128]{1,0:T(8,128)S(1)}, f32[768,128]{1,0:T(8,128)S(1)}) custom-call(f32[768,128]{1,0:T(8,128)S(1)} %bitcast.7, s32[2,8,128]{2,1,0:T(8,128)S(1)} %copy-done.3, s32[3,2,8,128]{3,2,1,0:T(8,128)S(1)} %copy-done.2, f32[4]{0:T(128)S(1)} %copy-done.4, f32[4]{0:T(128)S(1)} %copy-done.5, f32[2304,128]{1,0:T(8,128)S(1)} %bitcast.4), custom_call_target="tpu_custom_call" | custom-call | tf_op jit(solution)/shard_map/cavity/pallas_call | solution.py:476
  119.8 0.7 copy.10
  120.5 0.7 copy.11
Async XLA Ops:
  0.6 1.3 %copy-start = (f32[12,48,1,4,128]{4,3,2,1,0:T(4,128)S(1)}, f32[12,48,1,4,128]{4,3,2,1,0:T(4,128)}, u32[]{:S(2)}) copy-start(f32[12,48,1,4,128]{4,3,2,1,0:T(4,128)} %param.11) | copy-start | bytes 3538948
  1.9 1.0 copy-start.1
  2.9 0.7 copy-start.2
  3.6 0.7 copy-start.3
  4.3 0.7 copy-start.4
  5.0 0.7 copy-start.5

commit v2 on v1

--- a/solution.py
+++ b/solution.py
@@ -14,6 +14,7 @@
 NBRS = [(dx, dy) for dx in (-1, 0, 1) for dy in (-1, 0, 1) if (dx, dy) != (0, 0)]
 SX, SY, SZ = 2, 8, 128
 BASE = 64
+BLOCK = 16
 f32 = jnp.float32
 
 
@@ -27,6 +28,19 @@
 
 def tn(a, b):
     return lax.dot_general(a, b, (((0,), (0,)), ((), ())), precision=highest, preferred_element_type=f32)
+
+
+def split(a):
+    high = a.astype(jnp.bfloat16)
+    return high, (a - high.astype(f32)).astype(jnp.bfloat16)
+
+
+def nn3(a, b):
+    a_high, a_low = split(a)
+    b_high, b_low = split(b)
+    left = jnp.concatenate([a_high, a_low, a_high], axis=1)
+    right = jnp.concatenate([b_high, b_high, b_low], axis=0)
+    return lax.dot_general(left, right, (((1,), (0,)), ((), ())), preferred_element_type=f32)
 
 
 def lanes_of(shape):
@@ -53,14 +67,22 @@
 def eliminate(aug, full):
     shape = aug.shape
     row_at = rows_of(shape)
-    for j in range(V):
-        row = jnp.broadcast_to(aug[j : j + 1, :], shape)
-        col = jnp.broadcast_to(aug[:, BASE + j : BASE + j + 1], shape)
-        pivot = jnp.broadcast_to(aug[j : j + 1, BASE + j : BASE + j + 1], shape)
-        factor = jnp.where((row_at != j) if full else (row_at > j), col / pivot, 0.0)
-        aug = aug - factor * row
-    diag = jnp.sum(jnp.where(lanes_of(shape) == row_at + BASE, aug, 0.0), axis=1, keepdims=True)
-    return aug, jnp.broadcast_to(diag, shape)
+    recip = jnp.zeros(shape, f32)
+    for first in range(0, V, BLOCK):
+        cols = [
+            jnp.broadcast_to(aug[:, BASE + first + i : BASE + first + i + 1], shape) for i in range(BLOCK)
+        ]
+        rows = [aug[first + i : first + i + 1, :] for i in range(BLOCK)]
+        for i in range(BLOCK):
+            j = first + i
+            inv = 1.0 / cols[i][j : j + 1, :]
+            recip = jnp.where(row_at == j, inv, recip)
+            factor = jnp.where((row_at != j) if full else (row_at > j), cols[i] * inv, 0.0)
+            aug = aug - factor * rows[i]
+            for k in range(i + 1, BLOCK):
+                cols[k] = cols[k] - factor * cols[k][j : j + 1, :]
+                rows[k] = rows[k] - factor[first + k : first + k + 1, :] * rows[i]
+    return aug, recip
 
 
 def low_lanes(a, count):
@@ -79,13 +101,15 @@
 
 
 def solve_start(packed):
-    swept, diag = eliminate(packed, True)
-    ratio = low_lanes(swept / diag, V)
+    swept, recip = eliminate(packed, True)
+    return low_lanes(swept * recip, V)
+
+
+def invert_start(packed):
     stiff = low_lanes(packed, V)
     mass = low_lanes(pltpu.roll(packed, 128 - BASE, 1), V)
-    swept2, diag2 = eliminate(pltpu.roll(stiff, BASE, 1) + place(0), True)
-    inverse = low_lanes(swept2 / diag2, V)
-    return ratio, inverse, stiff, mass
+    swept, recip = eliminate(pltpu.roll(stiff, BASE, 1) + place(0), True)
+    return low_lanes(swept * recip, V), stiff, mass
 
 
 def project(work, packed, known, inv_known, stiff_known, mass_known, start):
@@ -94,7 +118,6 @@
     mass_row = low_lanes(pltpu.roll(packed, 128 - BASE, 1), total)
     spot = place(known)
     lanes = lanes_of((V, 128))
-    pad = 128 - known
 
     def square(known_part, row):
         corner = jnp.where(lanes < known, row, 0.0)
@@ -110,8 +133,9 @@
     own = pltpu.roll(own, (BASE - known) % 128, 1)
     schur = own - nt(reach, pad_rows(coupling, BASE, 128))
     joint = spot - reach
-    swept, diag = eliminate(schur + joint, True)
-    solved = low_lanes(swept / diag, total)
+    work[...] = schur
+    swept, recip = eliminate(work[...] + joint, True)
+    solved = low_lanes(swept * recip, total)
     inverse = inv_pad + tn(joint, solved)
     step = nn(mass, inverse)
     coeffs = start
@@ -119,22 +143,27 @@
         coeffs = nn(coeffs, step)
         weighted = nn(coeffs, mass)
         work[...] = nt(weighted, pad_rows(coeffs, BASE, 128))
-        swept, diag = eliminate(work[...] + coeffs, False)
-        coeffs = low_lanes(swept / jnp.sqrt(diag), total)
+        swept, recip = eliminate(work[...] + coeffs, False)
+        coeffs = low_lanes(swept * jnp.sqrt(recip), total)
     rayleigh = nt(nn(coeffs, stiff), pad_rows(coeffs, 0, 128))
     return coeffs, rayleigh, inverse, stiff, mass
 
 
 def kernel(
     geo,
+    x0_any,
+    region_any,
+    mask_any,
+    nu_any,
+    eps_any,
+    binv_any,
+    modes_ref,
+    resid_ref,
     x0_ref,
     region_ref,
     mask_ref,
     nu_tab,
     eps_tab,
-    binv_any,
-    modes_ref,
-    resid_ref,
     fx,
     fax,
     fw1,
@@ -155,13 +184,26 @@
     stage_sets, sizes, dims = geo
     n_stage = len(stage_sets)
     bufs = rest[: 3 * n_stage]
-    (halo_send, halo_recv, red_send, red_recv, binv_sem) = rest[3 * n_stage :]
+    (halo_send, halo_recv, red_send, red_recv, in_sem) = rest[3 * n_stage :]
     n_axial, n_trans = dims
     a_me, t_me = lax.axis_index("axial"), lax.axis_index("trans")
     me = {"x": a_me // 2, "c": a_me % 2, "z": t_me // sizes["y"], "y": t_me % sizes["y"]}
 
-    binv_copy = pltpu.make_async_copy(binv_any, binv, binv_sem)
-    binv_copy.start()
+    in_copies = []
+    for k, (source, target) in enumerate(
+        [
+            (region_any, region_ref),
+            (nu_any, nu_tab),
+            (eps_any, eps_tab),
+            (mask_any, mask_ref),
+            (x0_any, x0_ref),
+            (binv_any, binv),
+        ]
+    ):
+        copy = pltpu.make_async_copy(source, target, in_sem.at[k])
+        copy.start()
+        in_copies.append(copy)
+    binv_copy = in_copies.pop()
 
     def moved(offset):
         spot = dict(me)
@@ -193,6 +235,8 @@
             pl.semaphore_signal(barrier, inc=1, device_id=moved(o), device_id_type=MESH)
             greeted += 1
 
+    for copy in in_copies:
+        copy.wait()
     region = region_ref[...]
     nu = jnp.zeros(region.shape, f32)
     eps = jnp.zeros(region.shape, f32)
@@ -213,24 +257,24 @@
 
     pl.semaphore_wait(barrier, greeted)
 
+    def send(ref, which, k, dx, dy, ys):
+        sx = pl.ds(1, SX) if dx == 0 else pl.ds(1 if dx < 0 else SX, 1)
+        tx = pl.ds(1, SX) if dx == 0 else pl.ds(SX + 1 if dx < 0 else 0, 1)
+        sy = ys if dy == 0 else pl.ds(1 if dy < 0 else SY, 1)
+        ty = ys if dy == 0 else pl.ds(SY + 1 if dy < 0 else 0, 1)
+        copy = pltpu.make_async_remote_copy(
+            src_ref=ref.at[sx, sy],
+            dst_ref=ref.at[tx, ty],
+            send_sem=halo_send.at[which, k],
+            recv_sem=halo_recv.at[which, k],
+            device_id=neighbour(dx, dy),
+            device_id_type=MESH,
+        )
+        copy.start()
+        return copy
+
     def halo_start(ref, which):
-        copies = []
-        for k, (dx, dy) in enumerate(NBRS):
-            sx = pl.ds(1, SX) if dx == 0 else pl.ds(1 if dx < 0 else SX, 1)
-            tx = pl.ds(1, SX) if dx == 0 else pl.ds(SX + 1 if dx < 0 else 0, 1)
-            sy = pl.ds(1, SY) if dy == 0 else pl.ds(1 if dy < 0 else SY, 1)
-            ty = pl.ds(1, SY) if dy == 0 else pl.ds(SY + 1 if dy < 0 else 0, 1)
-            copy = pltpu.make_async_remote_copy(
-                src_ref=ref.at[sx, sy],
-                dst_ref=ref.at[tx, ty],
-                send_sem=halo_send.at[which, k],
-                recv_sem=halo_recv.at[which, k],
-                device_id=neighbour(dx, dy),
-                device_id_type=MESH,
-            )
-            copy.start()
-            copies.append(copy)
-        return copies
+        return [send(ref, which, k, dx, dy, pl.ds(1, SY)) for k, (dx, dy) in enumerate(NBRS)]
 
     def halo_finish(ref, copies):
         for copy in copies:
@@ -291,9 +335,7 @@
             value = reduce_finish(buf, copies)
             if s == 0 and halo is not None:
                 halo_copies = halo_start(halo[0], halo[1])
-        if halo is not None:
-            halo_finish(halo[0], halo_copies)
-        return value
+        return value, (halo_copies if halo is not None else None)
 
     def operate(src, dst):
         for x in range(SX + 1):
@@ -325,24 +367,36 @@
                 hy1 - hy(0) - hx1 + hx(0) + q0 - above
             )
 
-    def gram(fields, image, newest):
-        count = V * len(fields)
-        part[...] = jnp.zeros(part.shape, f32)
-
-        def body(y, carry):
-            left, right = [], []
-            for x in range(SX):
-                e = jnp.broadcast_to(epsb[x + 1, y + 1][0:1], (V, SZ))
-                for c in range(3):
-                    w = newest[x + 1, y + 1, c]
-                    left.append(jnp.concatenate([image[x + 1, y + 1, c], w * e], axis=0))
-                    right.append(jnp.concatenate([f[x + 1, y + 1, c] for f in fields], axis=0))
-            part[:, 0:count] += nt(jnp.concatenate(left, axis=1), jnp.concatenate(right, axis=1))
-            return carry
-
-        lax.fori_loop(0, SY, body, 0)
+    def rows_dot(left, right):
+        def piece(ys):
+            a, b = [], []
+            for y in ys:
+                for x in range(SX):
+                    e = jnp.broadcast_to(epsb[x + 1, y + 1][0:1], (V, SZ))
+                    for c in range(3):
+                        a.append(left[x + 1, y + 1, c])
+                        b.append(jnp.concatenate(right(x + 1, y + 1, c, e), axis=0))
+            return nt(jnp.concatenate(a, axis=1), jnp.concatenate(b, axis=1))
+
+        half = SY // 2
+        return piece(range(half)) + piece(range(half, SY))
+
+    def gram_ahead(fields, images, newest):
+        known = V * len(images)
+        part[:, 0 : 2 * known + V] = rows_dot(
+            newest,
+            lambda x, y, c, e: [f[x, y, c] for f in images] + [f[x, y, c] * e for f in fields],
+        )
         both = part[...]
-        return both[0:V] + pltpu.roll(both[V : 2 * V], BASE, 1)
+        lanes = lanes_of(both.shape)
+        mass = jnp.where(lanes >= BASE, pltpu.roll(jnp.where(lanes < 2 * known + V, both, 0.0), BASE - known, 1), 0.0)
+        part[...] = mass + (jnp.where(lanes < known, both, 0.0) if known else 0.0)
+
+    def gram_own(known, image, newest):
+        work[...] = jnp.zeros(work.shape, f32)
+        work[:, 0:V] = rows_dot(newest, lambda x, y, c, e: [image[x, y, c]])
+        own = work[...]
+        return part[...] + (pltpu.roll(own, known, 1) if known else own)
 
     def residual(rows, images, fields, rows_mass, y_range, x_range, store):
         coeffs = jnp.concatenate([rows, -rows_mass], axis=1)
@@ -357,7 +411,7 @@
                             [f[x, y, c] for f in images] + [f[x, y, c] * e for f in fields], axis=0
                         )
                     )
-            out = nn(coeffs, jnp.concatenate(pieces, axis=1))
+            out = nn3(coeffs, jnp.concatenate(pieces, axis=1))
             k = 0
             for x in x_range:
                 for c in range(3):
@@ -370,8 +424,9 @@
     def store_r(x, y, c, value):
         fr[x, y, c] = value
 
-    def precondition(dst):
-        for yb in range(SY // 2):
+    def precondition(dst, which):
+        copies = []
+        for yb in (0, SY // 2 - 1) + tuple(range(1, SY // 2 - 1)):
             acc = jnp.zeros((12, V, SZ), f32)
 
             def body(i, acc):
@@ -392,6 +447,15 @@
                         dst[1 + cx, 1 + 2 * yb + cy, c] = (
                             keep[cx, 2 * yb + cy, c] * acc[4 * c + 2 * cx + cy]
                         )
+            ready = pl.ds(1 + 2 * yb, 2)
+            faces = [(-1, 0), (1, 0)]
+            if yb == 0:
+                faces += [(0, -1), (-1, -1), (1, -1)]
+            if yb == SY // 2 - 1:
+                faces += [(0, 1), (-1, 1), (1, 1)]
+            for dx, dy in faces:
+                copies.append(send(dst, which, len(copies), dx, dy, ready))
+        return copies
 
     mat_copies = halo_start(mat, 0)
     x_copies = halo_start(fx, 1)
@@ -401,28 +465,37 @@
             if x <= SX and y <= SY:
                 nub[x, y] = jnp.broadcast_to(mat[x, y, 0:1, :], (V, SZ))
             epsb[x, y] = jnp.broadcast_to(mat[x, y, 1:2, :], (8, SZ))
+    gram_ahead([fx], [], fx)
     halo_finish(fx, x_copies)
 
     scale = 1.0 / (SX * SY * SZ * n_axial * n_trans)
     operate(fx, fax)
-    packed = reduce_all(gram([fx], fax, fx), 0, (fax, 2)) * scale
-    ratio, inverse, stiff, mass = solve_start(packed)
+    packed, ax_copies = reduce_all(gram_own(0, fax, fx), 0, (fax, 2))
+    packed = packed * scale
+    ratio = solve_start(packed)
     rows_mass = tn(ratio, place(0))[0:V, 0:V]
+    halo_finish(fax, ax_copies)
     binv_copy.wait()
     residual(place(0)[:, 0:V], [fax], [fx], rows_mass, (0, SY + 2), range(SX + 2), store_r)
-    precondition(fw1)
-    halo_finish(fw1, halo_start(fw1, 3))
+    w_copies = precondition(fw1, 3)
+    gram_ahead([fx, fw1], [fax], fw1)
+    inverse, stiff, mass = invert_start(packed)
+    halo_finish(fw1, w_copies)
     operate(fw1, faw1)
-    packed = reduce_all(gram([fx, fw1], faw1, fw1), 1, (faw1, 4)) * scale
+    packed, aw_copies = reduce_all(gram_own(V, faw1, fw1), 1, (faw1, 4))
+    packed = packed * scale
     coeffs, rayleigh, inverse, stiff, mass = project(work, packed, V, inverse, stiff, mass, place(0))
     weighted = nn(low_lanes(rayleigh, V), pad_rows(coeffs, 0, 128))
+    halo_finish(faw1, aw_copies)
     residual(
         coeffs[:, 0 : 2 * V], [fax, faw1], [fx, fw1], weighted[:, 0 : 2 * V], (0, SY + 2), range(SX + 2), store_r
     )
-    precondition(fw2)
-    halo_finish(fw2, halo_start(fw2, 5))
+    w_copies = precondition(fw2, 5)
+    gram_ahead([fx, fw1, fw2], [fax, faw1], fw2)
+    halo_finish(fw2, w_copies)
     operate(fw2, faw2)
-    packed = reduce_all(gram([fx, fw1, fw2], faw2, fw2), 2, None) * scale
+    packed, _ = reduce_all(gram_own(2 * V, faw2, fw2), 2, None)
+    packed = packed * scale
     coeffs, rayleigh, _, _, _ = project(
         work, packed, 2 * V, inverse[0 : 2 * V], stiff[0 : 2 * V], mass[0 : 2 * V], coeffs
     )
@@ -431,31 +504,22 @@
     def rows_at(c, x, y):
         return pl.ds(c * SX * SY + (x - 1) * SY + (y - 1), V, stride=3 * SX * SY)
 
-    def store_out(x, y, c, value):
-        resid_ref[rows_at(c, x, y), :] = value
-
     core_x = range(1, SX + 1)
-    residual(
-        coeffs[:, 0 : 3 * V],
-        [fax, faw1, faw2],
-        [fx, fw1, fw2],
-        weighted[:, 0 : 3 * V],
-        (1, SY + 1),
-        core_x,
-        store_out,
-    )
+    both = jnp.concatenate([coeffs, weighted], axis=0)[:, 0 : 3 * V]
+    rows = coeffs[:, 0 : 3 * V]
 
     def body(y, carry):
-        pieces = []
-        for x in core_x:
-            for c in range(3):
-                pieces.append(jnp.concatenate([f[x, y, c] for f in (fx, fw1, fw2)], axis=0))
-        out = nn(coeffs[:, 0 : 3 * V], jnp.concatenate(pieces, axis=1))
-        k = 0
-        for x in core_x:
-            for c in range(3):
-                modes_ref[rows_at(c, x, y), :] = out[:, k * SZ : (k + 1) * SZ]
-                k += 1
+        spots = [(x, c) for x in core_x for c in range(3)]
+        gather = lambda fields: jnp.concatenate(
+            [jnp.concatenate([f[x, y, c] for f in fields], axis=0) for x, c in spots], axis=1
+        )
+        own = nn3(both, gather((fx, fw1, fw2)))
+        image = nn3(rows, gather((fax, faw1, faw2)))
+        for k, (x, c) in enumerate(spots):
+            span = slice(k * SZ, (k + 1) * SZ)
+            modes_ref[rows_at(c, x, y), :] = own[0:V, span]
+            e = jnp.broadcast_to(epsb[x, y][0:1], (V, SZ))
+            resid_ref[rows_at(c, x, y), :] = image[:, span] - e * own[V:, span]
         return carry
 
     lax.fori_loop(1, SY + 1, body, 0)
@@ -472,13 +536,19 @@
         members.append(n)
     messages = sum(n - 1 for n in members)
     vmem = pl.BlockSpec(memory_space=pltpu.VMEM)
-    smem = pl.BlockSpec(memory_space=pltpu.SMEM)
     modes, resid = pl.pallas_call(
         functools.partial(kernel, geo),
         out_shape=[jax.ShapeDtypeStruct((V * 3 * SX * SY, SZ), f32)] * 2,
-        in_specs=[vmem, vmem, vmem, smem, smem, pl.BlockSpec(memory_space=pl.ANY)],
+        in_specs=[pl.BlockSpec(memory_space=pl.ANY)] * 6,
         out_specs=[vmem, vmem],
-        scratch_shapes=[ext] * 7
+        scratch_shapes=[
+            pltpu.VMEM((V * 3 * SX * SY, SZ), f32),
+            pltpu.VMEM((SX, SY, SZ), jnp.int32),
+            pltpu.VMEM((3, SX, SY, SZ), jnp.int32),
+            pltpu.SMEM((4,), f32),
+            pltpu.SMEM((4,), f32),
+        ]
+        + [ext] * 7
         + [
             pltpu.VMEM((SX + 1, SY + 1, 4, V, SZ), f32),
             pltpu.VMEM((SX + 2, SY + 2, 8, SZ), f32),
@@ -486,19 +556,19 @@
             pltpu.VMEM((SX + 1, SY + 1, V, SZ), f32),
             pltpu.VMEM((SX + 2, SY + 2, 8, SZ), f32),
             pltpu.VMEM((12 * 48 * SY // 2, SZ), f32),
-            pltpu.VMEM((2 * V, SZ), f32),
+            pltpu.VMEM((V, SZ), f32),
             pltpu.VMEM((V, 128), f32),
         ]
         + [pltpu.VMEM((n, V, SZ), f32) for _ in range(3) for n in members]
         + [
-            pltpu.SemaphoreType.DMA((6, 8)),
-            pltpu.SemaphoreType.DMA((6, 8)),
+            pltpu.SemaphoreType.DMA((6, 14)),
+            pltpu.SemaphoreType.DMA((6, 14)),
             pltpu.SemaphoreType.DMA((3, messages)),
             pltpu.SemaphoreType.DMA((3, messages)),
-            pltpu.SemaphoreType.DMA,
+            pltpu.SemaphoreType.DMA((6,)),
         ],
         compiler_params=pltpu.CompilerParams(
-            collective_id=0, has_side_effects=True, vmem_limit_bytes=48 * 1024 * 1024
+            collective_id=0, has_side_effects=True, vmem_limit_bytes=60 * 1024 * 1024
         ),
         name="cavity",
     )(
@@ -517,7 +587,7 @@
     n_axial, n_trans = mesh.shape["axial"], mesh.shape["trans"]
     y = 4 if n_trans % 16 == 0 else 2
     sizes = {"c": 2, "x": n_axial // 2, "z": n_trans // y, "y": y}
-    return (("c", "z"), ("x", "y")), sizes, (n_axial, n_trans)
+    return (("x", "y"), ("c", "z")), sizes, (n_axial, n_trans)
 
 
 def solution(mesh):

time: 122 us -> 96.3 us (0.79)
  Pallas kernels: 114 us -> 92 us
  local copies, waits for them, and re-layouts: 6.5 us -> 3.53 us
    pallas_call x1, Pallas kernels: 114 us -> 92 us  [on_device(): pl.pallas_call(functools.partial(kernel, geo), out_shape=[jax.ShapeDtypeS...]
    unnamed x14 -> x2, local copies, waits for them, and re-layouts: 6.5 us -> 3.53 us
where the time goes in v2:
time: 96.3 us; the launch traced here: 96.2 us
  Pallas kernels  92 us (96%)
  local copies, waits for them, and re-layouts  3.53 us (4%)
    pallas_call x1, Pallas kernels, on_device(): pl.pallas_call(functools.partial(kernel, geo), out_shape=[jax.ShapeDtypeS...  92 us
    unnamed x2, local copies, waits for them, and re-layouts  3.53 us

profile of v2, /device:TPU:1, one launch (start us, length us, event | category | flops | bytes accessed | tf_op | source)
XLA Modules:
  0.0 96.2 jit_solution(1611861925728701009)
XLA Ops:
  0.6 92.0 %cavity.1 = (f32[768,128]{1,0:T(8,128)}, f32[768,128]{1,0:T(8,128)}) custom-call(f32[768,128]{1,0:T(8,128)} %bitcast.7, s32[2,8,128]{2,1,0:T(8,128)} %region_any.1, s32[3,2,8,128]{3,2,1,0:T(8,128)} %mask_any.1, f32[4]{0:T(128)} %nu_any.1, f32[4]{0:T(128)} %eps_any.1, f32[2304,128]{1,0:T(8,128)} %bitcast.4), custom_call_target="tpu_custom_call" | custom-call | tf_op jit(solution)/shard_map/cavity/pallas_call | solution.py:539
  92.6 1.8 %copy.10 = f32[16,3,2,8,128]{4,3,2,1,0:T(8,128)} copy(f32[16,3,2,8,128]{4,3,2,1,0:T(8,128)} %bitcast.6) | data formatting | bytes 786432
  94.4 1.8 %copy.11 = f32[16,3,2,8,128]{4,3,2,1,0:T(8,128)} copy(f32[16,3,2,8,128]{4,3,2,1,0:T(8,128)} %bitcast.5) | data formatting | bytes 786432

commit v3 on v2

--- a/solution.py
+++ b/solution.py
@@ -171,6 +171,10 @@
     fw2,
     faw2,
     fr,
+    tax,
+    tmx,
+    taw,
+    tmw,
     flux,
     mat,
     keep,
@@ -329,13 +333,28 @@
             copy.wait_send()
         return value
 
-    def reduce_all(value, phase, halo):
+    def reduce_all(value, phase, ref=None, which=0, first=None, then=None):
+        width = V * (phase + 1)
+        dense = 4 * width <= 128
+        if dense:
+            value = value[0 : V // 2] + pltpu.roll(value[V // 2 : V], width, 1)
+        copies = None
         for s in range(n_stage):
-            buf, copies = reduce_stage(value, phase, s)
-            value = reduce_finish(buf, copies)
-            if s == 0 and halo is not None:
-                halo_copies = halo_start(halo[0], halo[1])
-        return value, (halo_copies if halo is not None else None)
+            buf, sent = reduce_stage(value, phase, s)
+            if s == 0:
+                if ref is not None:
+                    copies = halo_start(ref, which)
+                if first is not None:
+                    first()
+            elif then is not None:
+                then(copies)
+            value = reduce_finish(buf, sent)
+        if dense:
+            keep_lanes = lanes_of(value.shape) % BASE < width
+            low = jnp.where(keep_lanes, value, 0.0)
+            high = jnp.where(keep_lanes, pltpu.roll(value, 128 - width, 1), 0.0)
+            value = jnp.concatenate([low, high], axis=0)
+        return value
 
     def operate(src, dst):
         for x in range(SX + 1):
@@ -398,55 +417,41 @@
         own = work[...]
         return part[...] + (pltpu.roll(own, known, 1) if known else own)
 
-    def residual(rows, images, fields, rows_mass, y_range, x_range, store):
-        coeffs = jnp.concatenate([rows, -rows_mass], axis=1)
-
-        def body(y, carry):
-            pieces = []
-            for x in x_range:
+    def scaled(src):
+        for x in range(SX + 2):
+            for y in range(SY + 2):
                 e = jnp.broadcast_to(epsb[x, y][0:1], (V, SZ))
-                for c in range(3):
-                    pieces.append(
-                        jnp.concatenate(
-                            [f[x, y, c] for f in images] + [f[x, y, c] * e for f in fields], axis=0
-                        )
-                    )
-            out = nn3(coeffs, jnp.concatenate(pieces, axis=1))
-            k = 0
-            for x in x_range:
-                for c in range(3):
-                    store(x, y, c, out[:, k * SZ : (k + 1) * SZ])
-                    k += 1
-            return carry
-
-        lax.fori_loop(*y_range, body, 0)
-
-    def store_r(x, y, c, value):
-        fr[x, y, c] = value
-
-    def precondition(dst, which):
-        copies = []
-        for yb in (0, SY // 2 - 1) + tuple(range(1, SY // 2 - 1)):
-            acc = jnp.zeros((12, V, SZ), f32)
+                fr[x, y] = src[x, y] * e[None]
+
+    def schwarz(src, dst):
+        for yb in range(SY // 2):
 
             def body(i, acc):
                 c2 = i // 4
                 ox = i - 4 * c2
                 for oy in range(4):
-                    patch = fr[ox, 2 * yb + oy, c2]
-                    rows = [
-                        binv[pl.ds(a * 192 + i * 16 + oy * 4 + yb, 1), :] for a in range(12)
-                    ]
+                    patch = src[ox, 2 * yb + oy, c2]
+                    rows = [binv[pl.ds(a * 192 + i * 16 + oy * 4 + yb, 1), :] for a in range(12)]
                     acc = acc + jnp.stack([jnp.broadcast_to(r, (V, SZ)) * patch for r in rows])
                 return acc
 
-            acc = lax.fori_loop(0, 12, body, acc)
+            acc = lax.fori_loop(0, 12, body, jnp.zeros((12, V, SZ), f32))
             for c in range(3):
                 for cx in range(2):
                     for cy in range(2):
-                        dst[1 + cx, 1 + 2 * yb + cy, c] = (
-                            keep[cx, 2 * yb + cy, c] * acc[4 * c + 2 * cx + cy]
-                        )
+                        dst[cx, 2 * yb + cy, c] = keep[cx, 2 * yb + cy, c] * acc[4 * c + 2 * cx + cy]
+
+    def combine_send(dst, which, rows, images, rows_mass, fields):
+        coeffs = jnp.concatenate([rows, -rows_mass], axis=1)
+        copies = []
+        spots = [(x, k, c) for x in range(SX) for k in range(2) for c in range(3)]
+        for yb in (0, SY // 2 - 1) + tuple(range(1, SY // 2 - 1)):
+            pieces = [
+                jnp.concatenate([f[x, 2 * yb + k, c] for f in images + fields], axis=0) for x, k, c in spots
+            ]
+            out = nn3(coeffs, jnp.concatenate(pieces, axis=1))
+            for n, (x, k, c) in enumerate(spots):
+                dst[1 + x, 1 + 2 * yb + k, c] = out[:, n * SZ : (n + 1) * SZ]
             ready = pl.ds(1 + 2 * yb, 2)
             faces = [(-1, 0), (1, 0)]
             if yb == 0:
@@ -470,32 +475,41 @@
 
     scale = 1.0 / (SX * SY * SZ * n_axial * n_trans)
     operate(fx, fax)
-    packed, ax_copies = reduce_all(gram_own(0, fax, fx), 0, (fax, 2))
-    packed = packed * scale
+
+    def mass_start():
+        scaled(fx)
+        binv_copy.wait()
+        schwarz(fr, tmx)
+
+    def image_start(copies):
+        halo_finish(fax, copies)
+        schwarz(fax, tax)
+
+    packed = reduce_all(gram_own(0, fax, fx), 0, fax, 2, mass_start, image_start) * scale
     ratio = solve_start(packed)
     rows_mass = tn(ratio, place(0))[0:V, 0:V]
-    halo_finish(fax, ax_copies)
-    binv_copy.wait()
-    residual(place(0)[:, 0:V], [fax], [fx], rows_mass, (0, SY + 2), range(SX + 2), store_r)
-    w_copies = precondition(fw1, 3)
+    w_copies = combine_send(fw1, 3, place(0)[:, 0:V], [tax], rows_mass, [tmx])
     gram_ahead([fx, fw1], [fax], fw1)
     inverse, stiff, mass = invert_start(packed)
     halo_finish(fw1, w_copies)
     operate(fw1, faw1)
-    packed, aw_copies = reduce_all(gram_own(V, faw1, fw1), 1, (faw1, 4))
-    packed = packed * scale
+
+    def mass_next():
+        scaled(fw1)
+        schwarz(fr, tmw)
+
+    def image_next(copies):
+        halo_finish(faw1, copies)
+        schwarz(faw1, taw)
+
+    packed = reduce_all(gram_own(V, faw1, fw1), 1, faw1, 4, mass_next, image_next) * scale
     coeffs, rayleigh, inverse, stiff, mass = project(work, packed, V, inverse, stiff, mass, place(0))
     weighted = nn(low_lanes(rayleigh, V), pad_rows(coeffs, 0, 128))
-    halo_finish(faw1, aw_copies)
-    residual(
-        coeffs[:, 0 : 2 * V], [fax, faw1], [fx, fw1], weighted[:, 0 : 2 * V], (0, SY + 2), range(SX + 2), store_r
-    )
-    w_copies = precondition(fw2, 5)
+    w_copies = combine_send(fw2, 5, coeffs[:, 0 : 2 * V], [tax, taw], weighted[:, 0 : 2 * V], [tmx, tmw])
     gram_ahead([fx, fw1, fw2], [fax, faw1], fw2)
     halo_finish(fw2, w_copies)
     operate(fw2, faw2)
-    packed, _ = reduce_all(gram_own(2 * V, faw2, fw2), 2, None)
-    packed = packed * scale
+    packed = reduce_all(gram_own(2 * V, faw2, fw2), 2) * scale
     coeffs, rayleigh, _, _, _ = project(
         work, packed, 2 * V, inverse[0 : 2 * V], stiff[0 : 2 * V], mass[0 : 2 * V], coeffs
     )
@@ -508,21 +522,21 @@
     both = jnp.concatenate([coeffs, weighted], axis=0)[:, 0 : 3 * V]
     rows = coeffs[:, 0 : 3 * V]
 
-    def body(y, carry):
-        spots = [(x, c) for x in core_x for c in range(3)]
+    def body(yb, carry):
+        spots = [(x, 1 + 2 * yb + k, c) for x in core_x for k in range(2) for c in range(3)]
         gather = lambda fields: jnp.concatenate(
-            [jnp.concatenate([f[x, y, c] for f in fields], axis=0) for x, c in spots], axis=1
+            [jnp.concatenate([f[x, y, c] for f in fields], axis=0) for x, y, c in spots], axis=1
         )
         own = nn3(both, gather((fx, fw1, fw2)))
         image = nn3(rows, gather((fax, faw1, faw2)))
-        for k, (x, c) in enumerate(spots):
+        for k, (x, y, c) in enumerate(spots):
             span = slice(k * SZ, (k + 1) * SZ)
             modes_ref[rows_at(c, x, y), :] = own[0:V, span]
             e = jnp.broadcast_to(epsb[x, y][0:1], (V, SZ))
             resid_ref[rows_at(c, x, y), :] = image[:, span] - e * own[V:, span]
         return carry
 
-    lax.fori_loop(1, SY + 1, body, 0)
+    lax.fori_loop(0, SY // 2, body, 0)
 
 
 def on_device(geo, start_modes, region, edge_mask, reluctivity, permittivity, block_inverse):
@@ -549,6 +563,7 @@
             pltpu.SMEM((4,), f32),
         ]
         + [ext] * 7
+        + [pltpu.VMEM((SX, SY, 3, V, SZ), f32)] * 4
         + [
             pltpu.VMEM((SX + 1, SY + 1, 4, V, SZ), f32),
             pltpu.VMEM((SX + 2, SY + 2, 8, SZ), f32),
@@ -559,7 +574,7 @@
             pltpu.VMEM((V, SZ), f32),
             pltpu.VMEM((V, 128), f32),
         ]
-        + [pltpu.VMEM((n, V, SZ), f32) for _ in range(3) for n in members]
+        + [pltpu.VMEM((n, rows, SZ), f32) for rows in (V // 2, V // 2, V) for n in members]
         + [
             pltpu.SemaphoreType.DMA((6, 14)),
             pltpu.SemaphoreType.DMA((6, 14)),
@@ -587,7 +602,7 @@
     n_axial, n_trans = mesh.shape["axial"], mesh.shape["trans"]
     y = 4 if n_trans % 16 == 0 else 2
     sizes = {"c": 2, "x": n_axial // 2, "z": n_trans // y, "y": y}
-    return (("x", "y"), ("c", "z")), sizes, (n_axial, n_trans)
+    return (("c", "z"), ("x", "y")), sizes, (n_axial, n_trans)
 
 
 def solution(mesh):

time: 96.3 us -> 82.4 us (0.86)
  Pallas kernels: 92 us -> 78.1 us
    pallas_call x1, Pallas kernels: 92 us -> 78.1 us  [on_device(): pl.pallas_call(functools.partial(kernel, geo), out_shape=[jax.ShapeDtypeS...]
where the time goes in v3:
time: 82.4 us; the launch traced here: 82.2 us
  Pallas kernels  78.1 us (95%)
  local copies, waits for them, and re-layouts  3.53 us (4%)
    pallas_call x1, Pallas kernels, on_device(): pl.pallas_call(functools.partial(kernel, geo), out_shape=[jax.ShapeDtypeS...  78.1 us
    unnamed x2, local copies, waits for them, and re-layouts  3.53 us

profile of v3, /device:TPU:1, one launch (start us, length us, event | category | flops | bytes accessed | tf_op | source)
XLA Modules:
  0.0 82.2 jit_solution(12598870258332146561)
XLA Ops:
  0.6 78.1 %cavity.1 = (f32[768,128]{1,0:T(8,128)}, f32[768,128]{1,0:T(8,128)}) custom-call(f32[768,128]{1,0:T(8,128)} %bitcast.7, s32[2,8,128]{2,1,0:T(8,128)} %region_any.1, s32[3,2,8,128]{3,2,1,0:T(8,128)} %mask_any.1, f32[4]{0:T(128)} %nu_any.1, f32[4]{0:T(128)} %eps_any.1, f32[2304,128]{1,0:T(8,128)} %bitcast.4), custom_call_target="tpu_custom_call" | custom-call | tf_op jit(solution)/shard_map/cavity/pallas_call | solution.py:553
  78.7 1.8 %copy.10 = f32[16,3,2,8,128]{4,3,2,1,0:T(8,128)} copy(f32[16,3,2,8,128]{4,3,2,1,0:T(8,128)} %bitcast.6) | data formatting | bytes 786432
  80.5 1.8 %copy.11 = f32[16,3,2,8,128]{4,3,2,1,0:T(8,128)} copy(f32[16,3,2,8,128]{4,3,2,1,0:T(8,128)} %bitcast.5) | data formatting | bytes 786432

commit v4 on v3

--- a/solution.py
+++ b/solution.py
@@ -41,6 +41,14 @@
     left = jnp.concatenate([a_high, a_low, a_high], axis=1)
     right = jnp.concatenate([b_high, b_high, b_low], axis=0)
     return lax.dot_general(left, right, (((1,), (0,)), ((), ())), preferred_element_type=f32)
+
+
+def nt3(a, b):
+    a_high, a_low = split(a)
+    b_high, b_low = split(b)
+    left = jnp.concatenate([a_high, a_low, a_high], axis=1)
+    right = jnp.concatenate([b_high, b_high, b_low], axis=1)
+    return lax.dot_general(left, right, (((1,), (1,)), ((), ())), preferred_element_type=f32)
 
 
 def lanes_of(shape):
@@ -98,6 +106,47 @@
     if after:
         parts.append(jnp.zeros((after, 128), f32))
     return jnp.concatenate(parts, axis=0) if len(parts) > 1 else a
+
+
+def fold(value, width):
+    half = value.shape[0] // 2
+    return value[0:half] + pltpu.roll(value[half:], width, 1)
+
+
+def unfold(value, width):
+    used = lanes_of(value.shape) % BASE < width
+    low = jnp.where(used, value, 0.0)
+    high = jnp.where(used, pltpu.roll(value, 128 - width, 1), 0.0)
+    return jnp.concatenate([low, high], axis=0)
+
+
+def pack(value, phase):
+    if phase == 0:
+        return fold(fold(value, V), 2 * V)
+    if phase == 1:
+        return fold(value, 2 * V)
+    low, high = value[0:8], value[8:16]
+    place_in = lanes_of(high.shape) % BASE
+    first = low + pltpu.roll(jnp.where(place_in < V, high, 0.0), 3 * V, 1)
+    rest = jnp.where((place_in >= V) & (place_in < 3 * V), high, 0.0)
+    return jnp.concatenate([first, rest[0:4] + pltpu.roll(rest[4:8], 2 * V, 1)], axis=0)
+
+
+def unpack(value, phase):
+    if phase == 0:
+        return unfold(unfold(value, 2 * V), V)
+    if phase == 1:
+        return unfold(value, 2 * V)
+    first, second = value[0:8], value[8:12]
+    place_in = lanes_of(first.shape) % BASE
+    low = jnp.where(place_in < 3 * V, first, 0.0)
+    high = jnp.where(place_in < V, pltpu.roll(first, 128 - 3 * V, 1), 0.0)
+    here = lanes_of(second.shape) % BASE
+    middle = (here >= V) & (here < 3 * V)
+    rest = jnp.concatenate(
+        [jnp.where(middle, second, 0.0), jnp.where(middle, pltpu.roll(second, 128 - 2 * V, 1), 0.0)], axis=0
+    )
+    return jnp.concatenate([low, high + rest], axis=0)
 
 
 def solve_start(packed):
@@ -219,9 +268,10 @@
         return (lax.rem(a_me + dx + n_axial, n_axial), lax.rem(t_me + dy + n_trans, n_trans))
 
     def offsets(stage):
-        return [
+        every = [
             dict(zip(stage, o)) for o in itertools.product(*[range(sizes[d]) for d in stage]) if any(o)
         ]
+        return sorted(every, key=lambda o: -sum(min(o[d], sizes[d] - o[d]) for d in o))
 
     def rank(stage):
         r = 0
@@ -334,10 +384,7 @@
         return value
 
     def reduce_all(value, phase, ref=None, which=0, first=None, then=None):
-        width = V * (phase + 1)
-        dense = 4 * width <= 128
-        if dense:
-            value = value[0 : V // 2] + pltpu.roll(value[V // 2 : V], width, 1)
+        value = pack(value, phase)
         copies = None
         for s in range(n_stage):
             buf, sent = reduce_stage(value, phase, s)
@@ -349,12 +396,7 @@
             elif then is not None:
                 then(copies)
             value = reduce_finish(buf, sent)
-        if dense:
-            keep_lanes = lanes_of(value.shape) % BASE < width
-            low = jnp.where(keep_lanes, value, 0.0)
-            high = jnp.where(keep_lanes, pltpu.roll(value, 128 - width, 1), 0.0)
-            value = jnp.concatenate([low, high], axis=0)
-        return value
+        return unpack(value, phase)
 
     def operate(src, dst):
         for x in range(SX + 1):
@@ -386,7 +428,7 @@
                 hy1 - hy(0) - hx1 + hx(0) + q0 - above
             )
 
-    def rows_dot(left, right):
+    def rows_dot(product, left, right):
         def piece(ys):
             a, b = [], []
             for y in ys:
@@ -395,7 +437,7 @@
                     for c in range(3):
                         a.append(left[x + 1, y + 1, c])
                         b.append(jnp.concatenate(right(x + 1, y + 1, c, e), axis=0))
-            return nt(jnp.concatenate(a, axis=1), jnp.concatenate(b, axis=1))
+            return product(jnp.concatenate(a, axis=1), jnp.concatenate(b, axis=1))
 
         half = SY // 2
         return piece(range(half)) + piece(range(half, SY))
@@ -403,6 +445,7 @@
     def gram_ahead(fields, images, newest):
         known = V * len(images)
         part[:, 0 : 2 * known + V] = rows_dot(
+            nt,
             newest,
             lambda x, y, c, e: [f[x, y, c] for f in images] + [f[x, y, c] * e for f in fields],
         )
@@ -413,7 +456,7 @@
 
     def gram_own(known, image, newest):
         work[...] = jnp.zeros(work.shape, f32)
-        work[:, 0:V] = rows_dot(newest, lambda x, y, c, e: [image[x, y, c]])
+        work[:, 0:V] = rows_dot(nt3, newest, lambda x, y, c, e: [image[x, y, c]])
         own = work[...]
         return part[...] + (pltpu.roll(own, known, 1) if known else own)
 
@@ -552,7 +595,7 @@
     vmem = pl.BlockSpec(memory_space=pltpu.VMEM)
     modes, resid = pl.pallas_call(
         functools.partial(kernel, geo),
-        out_shape=[jax.ShapeDtypeStruct((V * 3 * SX * SY, SZ), f32)] * 2,
+        out_shape=[pltpu.VMEM((V * 3 * SX * SY, SZ), f32)] * 2,
         in_specs=[pl.BlockSpec(memory_space=pl.ANY)] * 6,
         out_specs=[vmem, vmem],
         scratch_shapes=[
@@ -574,7 +617,7 @@
             pltpu.VMEM((V, SZ), f32),
             pltpu.VMEM((V, 128), f32),
         ]
-        + [pltpu.VMEM((n, rows, SZ), f32) for rows in (V // 2, V // 2, V) for n in members]
+        + [pltpu.VMEM((n, rows, SZ), f32) for rows in (4, 8, 12) for n in members]
         + [
             pltpu.SemaphoreType.DMA((6, 14)),
             pltpu.SemaphoreType.DMA((6, 14)),

time: 82.4 us -> 75.7 us (0.919)
  Pallas kernels: 78.1 us -> 73.5 us
  local copies, waits for them, and re-layouts: 3.53 us -> 1.49 us
    pallas_call x1, Pallas kernels: 78.1 us -> 73.5 us  [on_device(): pl.pallas_call(functools.partial(kernel, geo), out_shape=[pltpu.VMEM((V *...]
    unnamed x2, local copies, waits for them, and re-layouts: 3.53 us -> 1.49 us
where the time goes in v4:
time: 75.7 us; the launch traced here: 75.6 us
  Pallas kernels  73.5 us (97%)
  local copies, waits for them, and re-layouts  1.49 us (2%)
    pallas_call x1, Pallas kernels, on_device(): pl.pallas_call(functools.partial(kernel, geo), out_shape=[pltpu.VMEM((V *...  73.5 us

profile of v4, /device:TPU:1, one launch (start us, length us, event | category | flops | bytes accessed | tf_op | source)
XLA Modules:
  0.0 75.6 jit_solution(7722604675185246234)
XLA Ops:
  0.6 73.5 %cavity.1 = (f32[768,128]{1,0:T(8,128)S(1)}, f32[768,128]{1,0:T(8,128)S(1)}) custom-call(f32[768,128]{1,0:T(8,128)} %bitcast.7, s32[2,8,128]{2,1,0:T(8,128)} %region_any.1, s32[3,2,8,128]{3,2,1,0:T(8,128)} %mask_any.1, f32[4]{0:T(128)} %nu_any.1, f32[4]{0:T(128)} %eps_any.1, f32[2304,128]{1,0:T(8,128)} %bitcast.6), custom_call_target="tpu_custom_call" | custom-call | tf_op jit(solution)/shard_map/cavity/pallas_call | solution.py:596
  74.1 0.7 copy.10
  74.9 0.7 copy.11

commit v5 on v4

--- a/solution.py
+++ b/solution.py
@@ -242,6 +242,37 @@
     a_me, t_me = lax.axis_index("axial"), lax.axis_index("trans")
     me = {"x": a_me // 2, "c": a_me % 2, "z": t_me // sizes["y"], "y": t_me % sizes["y"]}
 
+    def moved(offset):
+        spot = dict(me)
+        for d in offset:
+            spot[d] = lax.rem(me[d] + offset[d], sizes[d])
+        return (spot["x"] * 2 + spot["c"], spot["z"] * sizes["y"] + spot["y"])
+
+    def neighbour(dx, dy):
+        return (lax.rem(a_me + dx + n_axial, n_axial), lax.rem(t_me + dy + n_trans, n_trans))
+
+    def offsets(stage):
+        every = [
+            dict(zip(stage, o)) for o in itertools.product(*[range(sizes[d]) for d in stage]) if any(o)
+        ]
+        return sorted(every, key=lambda o: -sum(min(o[d], sizes[d] - o[d]) for d in o))
+
+    def rank(stage):
+        r = 0
+        for d in stage:
+            r = r * sizes[d] + me[d]
+        return r
+
+    barrier = pltpu.get_barrier_semaphore()
+    greeted = 0
+    for stage in stage_sets:
+        for o in offsets(stage):
+            pl.semaphore_signal(barrier, inc=1, device_id=moved(o), device_id_type=MESH)
+            greeted += 1
+    for dx, dy in NBRS:
+        pl.semaphore_signal(barrier, inc=1, device_id=neighbour(dx, dy), device_id_type=MESH)
+        greeted += 1
+
     in_copies = []
     for k, (source, target) in enumerate(
         [
@@ -257,37 +288,6 @@
         copy.start()
         in_copies.append(copy)
     binv_copy = in_copies.pop()
-
-    def moved(offset):
-        spot = dict(me)
-        for d in offset:
-            spot[d] = lax.rem(me[d] + offset[d], sizes[d])
-        return (spot["x"] * 2 + spot["c"], spot["z"] * sizes["y"] + spot["y"])
-
-    def neighbour(dx, dy):
-        return (lax.rem(a_me + dx + n_axial, n_axial), lax.rem(t_me + dy + n_trans, n_trans))
-
-    def offsets(stage):
-        every = [
-            dict(zip(stage, o)) for o in itertools.product(*[range(sizes[d]) for d in stage]) if any(o)
-        ]
-        return sorted(every, key=lambda o: -sum(min(o[d], sizes[d] - o[d]) for d in o))
-
-    def rank(stage):
-        r = 0
-        for d in stage:
-            r = r * sizes[d] + me[d]
-        return r
-
-    barrier = pltpu.get_barrier_semaphore()
-    greeted = 0
-    for dx, dy in NBRS:
-        pl.semaphore_signal(barrier, inc=1, device_id=neighbour(dx, dy), device_id_type=MESH)
-        greeted += 1
-    for stage in stage_sets:
-        for o in offsets(stage):
-            pl.semaphore_signal(barrier, inc=1, device_id=moved(o), device_id_type=MESH)
-            greeted += 1
 
     for copy in in_copies:
         copy.wait()
@@ -565,7 +565,7 @@
     both = jnp.concatenate([coeffs, weighted], axis=0)[:, 0 : 3 * V]
     rows = coeffs[:, 0 : 3 * V]
 
-    def body(yb, carry):
+    for yb in range(SY // 2):
         spots = [(x, 1 + 2 * yb + k, c) for x in core_x for k in range(2) for c in range(3)]
         gather = lambda fields: jnp.concatenate(
             [jnp.concatenate([f[x, y, c] for f in fields], axis=0) for x, y, c in spots], axis=1
@@ -577,9 +577,6 @@
             modes_ref[rows_at(c, x, y), :] = own[0:V, span]
             e = jnp.broadcast_to(epsb[x, y][0:1], (V, SZ))
             resid_ref[rows_at(c, x, y), :] = image[:, span] - e * own[V:, span]
-        return carry
-
-    lax.fori_loop(0, SY // 2, body, 0)
 
 
 def on_device(geo, start_modes, region, edge_mask, reluctivity, permittivity, block_inverse):
@@ -609,7 +606,7 @@
         + [pltpu.VMEM((SX, SY, 3, V, SZ), f32)] * 4
         + [
             pltpu.VMEM((SX + 1, SY + 1, 4, V, SZ), f32),
-            pltpu.VMEM((SX + 2, SY + 2, 8, SZ), f32),
+            pltpu.VMEM((SX + 2, SY + 2, 2, SZ), f32),
             pltpu.VMEM((SX, SY, 3, V, SZ), f32),
             pltpu.VMEM((SX + 1, SY + 1, V, SZ), f32),
             pltpu.VMEM((SX + 2, SY + 2, 8, SZ), f32),

time: 75.7 us -> 75.4 us (level)
  no operation moved by 1% of the time
where the time goes in v5:
time: 75.4 us; the launch traced here: 75.3 us
  Pallas kernels  73.2 us (97%)
  local copies, waits for them, and re-layouts  1.49 us (2%)
    pallas_call x1, Pallas kernels, on_device(): pl.pallas_call(functools.partial(kernel, geo), out_shape=[pltpu.VMEM((V *...  73.2 us

profile of v5, /device:TPU:1, one launch (start us, length us, event | category | flops | bytes accessed | tf_op | source)
XLA Modules:
  0.0 75.3 jit_solution(2157763306855034075)
XLA Ops:
  0.6 73.2 %cavity.1 = (f32[768,128]{1,0:T(8,128)S(1)}, f32[768,128]{1,0:T(8,128)S(1)}) custom-call(f32[768,128]{1,0:T(8,128)} %bitcast.7, s32[2,8,128]{2,1,0:T(8,128)} %region_any.1, s32[3,2,8,128]{3,2,1,0:T(8,128)} %mask_any.1, f32[4]{0:T(128)} %nu_any.1, f32[4]{0:T(128)} %eps_any.1, f32[2304,128]{1,0:T(8,128)} %bitcast.6), custom_call_target="tpu_custom_call" | custom-call | tf_op jit(solution)/shard_map/cavity/pallas_call | solution.py:593
  73.8 0.7 copy.10
  74.6 0.7 copy.11

commit v6 on v5

--- a/solution.py
+++ b/solution.py
@@ -188,9 +188,11 @@
     inverse = inv_pad + tn(joint, solved)
     step = nn(mass, inverse)
     coeffs = start
+    step_mass = nn(step, mass)
     for repeat in range(INNER):
-        coeffs = nn(coeffs, step)
-        weighted = nn(coeffs, mass)
+        before = coeffs
+        coeffs = nn(before, step)
+        weighted = nn(before, step_mass) if repeat else nn(coeffs, mass)
         work[...] = nt(weighted, pad_rows(coeffs, BASE, 128))
         swept, recip = eliminate(work[...] + coeffs, False)
         coeffs = low_lanes(swept * jnp.sqrt(recip), total)

time: 75.4 us -> 75.4 us (level)
  no operation moved by 1% of the time
where the time goes in v6:
time: 75.4 us; the launch traced here: 75.2 us
  Pallas kernels  73.1 us (97%)
  local copies, waits for them, and re-layouts  1.49 us (2%)
    pallas_call x1, Pallas kernels, on_device(): pl.pallas_call(functools.partial(kernel, geo), out_shape=[pltpu.VMEM((V *...  73.1 us

profile of v6, /device:TPU:1, one launch (start us, length us, event | category | flops | bytes accessed | tf_op | source)
XLA Modules:
  0.0 75.2 jit_solution(2764524808288852741)
XLA Ops:
  0.6 73.1 %cavity.1 = (f32[768,128]{1,0:T(8,128)S(1)}, f32[768,128]{1,0:T(8,128)S(1)}) custom-call(f32[768,128]{1,0:T(8,128)} %bitcast.7, s32[2,8,128]{2,1,0:T(8,128)} %region_any.1, s32[3,2,8,128]{3,2,1,0:T(8,128)} %mask_any.1, f32[4]{0:T(128)} %nu_any.1, f32[4]{0:T(128)} %eps_any.1, f32[2304,128]{1,0:T(8,128)} %bitcast.6), custom_call_target="tpu_custom_call" | custom-call | tf_op jit(solution)/shard_map/cavity/pallas_call | solution.py:595
  73.7 0.7 copy.10
  74.5 0.7 copy.11
